TPU v7x, 32 devices: a whole 2x2x4 slice. The times are simulated.
32 devices in a mesh: dp: 16 (over z, x, core), group: 2 (over y).
Axes of the slice: x: 2, y: 2, z: 4, core: 2. Of those that a mesh axis runs over, the one named last changes fastest.
Arguments:
- queries: bfloat16 [4096, 256], P('dp'), may hold values from -110 to 110
- item_features: bfloat16 [4096, 2048], P('dp', 'group'), may hold values from -6 to 6
- corpus: bfloat16 [32768, 2048], P('dp', 'group'), may hold values from -6 to 6
- sample_ids: int32 [16384], P('dp'), may hold values from 0 to 2047
- sample_shift: bfloat16 [16384], P('dp'), may hold values from -2 to 2
- w1: bfloat16 [2048, 1024], P(None, 'group'), may hold values from -0.125 to 0.125
- w2: bfloat16 [1024, 256], P('group'), may hold values from -0.1875 to 0.1875
Outputs:
- query_loss: float32 [4096], P(('dp', 'group'))
- grad_query: float32 [4096, 256], P(('dp', 'group'))
- grad_w1: float32 [2048, 1024], P(None, 'group')
- grad_w2: float32 [1024, 256], P('group')
Inputs may be any that keep to these rules, and one draw needn't show every extreme that they name: sample_ids[k] is a row of the corpus block of the dp index that holds position k.
All inputs are finite; a program needn't handle non-finite values.
Results may differ from a plain program's by a relative error of at most 0.02.
The roundings to bfloat16 on the way count: a program that leaves them out, or rounds other values in their place, can miss the bound.
Values may be sent and summed in bfloat16 or wider, within the bound.
A program may use at most 128 MiB of HBM per device.

v0:
```python
import functools

import jax
import jax.numpy as jnp
from jax import lax
from jax.experimental import pallas as pl
from jax.experimental.pallas import tpu as pltpu
from jax.sharding import PartitionSpec as P

F32 = jnp.float32
BF16 = jnp.bfloat16
MESH = pl.DeviceIdType.MESH
ANY = pl.BlockSpec(memory_space=pl.ANY)
VMEM = pl.BlockSpec(memory_space=pltpu.VMEM)


def mm(a, b):
    return jnp.dot(a, b, preferred_element_type=F32)


def bits_of(n):
    return [1 << i for i in range(n.bit_length() - 1)]


def partner(axis, step):
    i = lax.axis_index(axis)
    bit = lax.rem(lax.div(i, step), 2)
    return bit, {axis: i + step - 2 * step * bit}


def greet(peers):
    barrier = pltpu.get_barrier_semaphore()
    for peer in peers:
        pl.semaphore_signal(barrier, inc=1, device_id=peer, device_id_type=MESH)
    pl.semaphore_wait(barrier, len(peers))


def score_kernel(groups, n_dp, local, queries_in, normed, normed_t, bias,
                 total_ref, hat_ref, part_ref, rest_ref,
                 queries, logits, stats, arrived, qsem, send_sem, recv_sem, fsend, frecv):
    tiles, cols, width = logits.shape
    emb = normed.shape[1]
    scale = emb ** (-0.5)
    member = lax.axis_index("group")
    rounds = [("dp", b) for b in bits_of(n_dp)] + [("group", b) for b in bits_of(groups)]
    peers = [partner(a, b)[1] for a, b in rounds]
    others = [lax.rem(member + s, groups) for s in range(1, groups)]
    extra = [{"group": o} for o in others] if groups > 2 else []
    fetch = pltpu.make_async_copy(queries_in, queries, qsem)
    fetch.start()
    greet(peers + extra)
    copies = []
    for s in range(1, groups):
        for t in range(1, groups):
            k = (s - 1) * (groups - 1) + t - 1
            copy = pltpu.make_async_remote_copy(
                src_ref=local.at[(s + t) % groups],
                dst_ref=rest_ref.at[s - 1, t - 1],
                send_sem=fsend.at[k], recv_sem=frecv.at[k],
                device_id={"group": others[s - 1]}, device_id_type=MESH)
            copy.start()
            copies.append(copy)

    def first(i, carry):
        q = queries[pl.ds(pl.multiple_of(i * width, width), width), :]
        block = scale * lax.dot_general(
            normed[...], q, (((1,), (1,)), ((), ())), preferred_element_type=F32) + bias[...]
        logits[i] = block
        top = jnp.max(block, 0, keepdims=True)
        stats[0, 0, pl.ds(i, 1), :] = top
        stats[0, 1, pl.ds(i, 1), :] = jnp.sum(jnp.exp(block - top), 0, keepdims=True)
        return carry

    fetch.wait()
    lax.fori_loop(0, tiles, first, 0)
    for r, peer in enumerate(peers):
        copy = pltpu.make_async_remote_copy(
            src_ref=stats.at[r], dst_ref=arrived.at[r],
            send_sem=send_sem.at[r], recv_sem=recv_sem.at[r],
            device_id=peer, device_id_type=MESH)
        copy.start()
        copy.wait()
        m0, s0, m1, s1 = stats[r, 0], stats[r, 1], arrived[r, 0], arrived[r, 1]
        top = jnp.maximum(m0, m1)
        stats[r + 1, 0] = top
        stats[r + 1, 1] = s0 * jnp.exp(m0 - top) + s1 * jnp.exp(m1 - top)
    last = len(peers)
    total_ref[...] = stats[last, 0] + jnp.log(stats[last, 1])
    hat_ref[...] = jnp.zeros_like(hat_ref)

    def second(i, carry):
        at_i = pl.ds(pl.multiple_of(i * width, width), width)
        p = jnp.exp(logits[i] - total_ref[pl.ds(i, 1), :]).astype(BF16)
        hat_ref[...] += mm(p, queries[at_i, :])
        part_ref[at_i, :] = mm(normed_t[...], p).T
        return carry

    lax.fori_loop(0, tiles, second, 0)
    for copy in copies:
        copy.wait()


def score(groups, n_dp, local, queries, normed, bias):
    rows, fg = local.shape[1:]
    width = 256
    total, emb = queries.shape
    tiles = total // width
    rounds = len(bits_of(n_dp)) + len(bits_of(groups))
    n_copies = (groups - 1) ** 2
    return pl.pallas_call(
        functools.partial(score_kernel, groups, n_dp),
        out_shape=(
            jax.ShapeDtypeStruct((tiles, width), F32),
            jax.ShapeDtypeStruct((rows, emb), F32),
            jax.ShapeDtypeStruct((total, emb), F32),
            jax.ShapeDtypeStruct((groups - 1, groups - 1, rows, fg), BF16),
        ),
        in_specs=[ANY, ANY, VMEM, VMEM, VMEM],
        out_specs=(VMEM, VMEM, VMEM, ANY),
        scratch_shapes=[
            pltpu.VMEM((total, emb), BF16),
            pltpu.VMEM((tiles, rows, width), F32),
            pltpu.VMEM((rounds + 1, 2, tiles, width), F32),
            pltpu.VMEM((rounds, 2, tiles, width), F32),
            pltpu.SemaphoreType.DMA,
            pltpu.SemaphoreType.DMA((rounds,)),
            pltpu.SemaphoreType.DMA((rounds,)),
            pltpu.SemaphoreType.DMA((n_copies,)),
            pltpu.SemaphoreType.DMA((n_copies,)),
        ],
        compiler_params=pltpu.CompilerParams(
            collective_id=0, has_side_effects=True, vmem_limit_bytes=44 << 20),
        name="score",
    )(local, queries, normed, normed.T, bias)


def reduce_kernel(plans, n_in, n_peers_of, *refs):
    n = len(plans)
    ins, refs = refs[:n_in], refs[n_in:]
    outs = refs[:n]
    accs, sends, recvs = (refs[n + i * n : 2 * n + i * n] for i in range(3))
    send_sem, recv_sem, gsend, grecv = refs[4 * n :]
    greet([partner(a, b)[1] for a, b in n_peers_of])
    live = {}

    def begin(i, r):
        rounds, bases, _, source, start, count = plans[i]
        bit, peer = partner(*rounds[r])
        half = count >> (r + 1)
        at0 = count - 2 * half

        def stage(j, carry):
            if r == 0:
                block = ins[source][start + bases(j) + (1 - bit) * bases(half)]
            else:
                block = accs[i][(1 - bit) * half + j]
            sends[i][at0 + j] = block.astype(BF16)
            return carry

        lax.fori_loop(0, half, stage, 0)
        copy = pltpu.make_async_remote_copy(
            src_ref=sends[i].at[pl.ds(at0, half)], dst_ref=recvs[i].at[pl.ds(at0, half)],
            send_sem=send_sem.at[i, r], recv_sem=recv_sem.at[i, r],
            device_id=peer, device_id_type=MESH)
        copy.start()
        live[i] = copy

    def finish(i, r):
        rounds, bases, _, source, start, count = plans[i]
        bit, _ = partner(*rounds[r])
        half = count >> (r + 1)
        at0 = count - 2 * half
        live[i].wait()

        def add(j, carry):
            if r == 0:
                block = ins[source][start + bases(j) + bit * bases(half)]
            else:
                block = accs[i][bit * half + j]
            accs[i][j] = block + recvs[i][at0 + j].astype(F32)
            return carry

        lax.fori_loop(0, half, add, 0)

    def place(i, r):
        rounds = plans[i][0]
        return sum(partner(*rounds[k])[0] * (plans[i][5] >> (k + 1)) for k in range(r + 1))

    def share(i, r):
        peer = partner(*plans[i][0][r])[1]
        span = pl.ds(place(i, r), plans[i][5] >> (r + 1))
        copy = pltpu.make_async_remote_copy(
            src_ref=outs[i].at[span], dst_ref=outs[i].at[span],
            send_sem=gsend.at[i, r], recv_sem=grecv.at[i, r],
            device_id=peer, device_id_type=MESH)
        copy.start()
        live[i] = copy

    def advance(i, step):
        rounds, _, gather = plans[i][:3]
        k = len(rounds)
        if 0 < step <= k:
            finish(i, step - 1)
        if step < k:
            begin(i, step)
        elif step == k and not gather:
            outs[i][0] = accs[i][0]
        elif gather and step <= 2 * k:
            if step == k:
                outs[i][place(i, k - 1)] = accs[i][0].astype(BF16)
            else:
                live[i].wait()
            if step < 2 * k:
                share(i, 2 * k - 1 - step)

    steps = max(len(p[0]) * (2 if p[2] else 1) for p in plans) + 1
    for step in range(steps):
        for i in range(n):
            advance(i, step)


def bit_place(steps, j):
    k = len(steps)
    out = 0
    for i, step in enumerate(steps):
        weight = 1 << (k - 1 - i)
        if isinstance(j, int):
            out += (j // weight) % 2 * step
        else:
            out = out + lax.rem(lax.div(j, weight), 2) * step
    return out


def reduce_all(groups, n_dp, xs, parts):
    plans = []
    for source, start, n, rounds, gather in parts:
        if gather:
            steps = [n >> (k + 1) for k in range(len(rounds))]
        else:
            steps = [b * groups if a == "dp" else b for a, b in rounds]
        bases = functools.partial(bit_place, steps)
        plans.append((rounds, bases, gather, source, start, n))
    shapes = [(p[5],) + xs[p[3]].shape[1:] for p in plans]
    most = max(len(p[0]) for p in plans)
    peers = [("dp", b) for b in bits_of(n_dp)] + [("group", b) for b in bits_of(groups)]
    sems = pltpu.SemaphoreType.DMA((len(plans), most))
    return pl.pallas_call(
        functools.partial(reduce_kernel, plans, len(xs), peers),
        out_shape=tuple(
            jax.ShapeDtypeStruct(shape, BF16) if p[2] else jax.ShapeDtypeStruct((1,) + shape[1:], F32)
            for shape, p in zip(shapes, plans)),
        in_specs=[VMEM] * len(xs),
        out_specs=(VMEM,) * len(plans),
        scratch_shapes=[pltpu.VMEM((s[0] // 2,) + s[1:], F32) for s in shapes]
        + [pltpu.VMEM(s, BF16) for s in shapes] * 2 + [sems] * 4,
        compiler_params=pltpu.CompilerParams(
            collective_id=1, has_side_effects=True, vmem_limit_bytes=48 << 20),
        name="reduce_all",
    )(*xs)


def per_device(queries, item_features, corpus, sample_ids, sample_shift, w1, w2):
    groups = lax.axis_size("group")
    member = lax.axis_index("group")
    n_dp = lax.axis_size("dp")
    d = lax.axis_index("dp")
    query_rows, emb = queries.shape
    quota = query_rows // groups
    negs = sample_ids.shape[0] // groups
    rows = quota + negs
    fg = item_features.shape[1]
    scale = emb ** (-0.5)

    def shift(x, s):
        return lax.ppermute(x, "group", [(i, (i + s) % groups) for i in range(groups)])

    def at(x, i):
        return lax.dynamic_index_in_dim(x, lax.rem(i, groups), 0, keepdims=False)

    def place_columns(parts):
        if groups == 2:
            swap = member == 0
            return jnp.concatenate(
                [jnp.where(swap, parts[0], parts[1]), jnp.where(swap, parts[1], parts[0])], 1)
        out = jnp.zeros((parts[0].shape[0], groups * fg), BF16)
        for s in range(groups):
            start = lax.rem(member + groups - s, groups) * fg
            out = lax.dynamic_update_slice_in_dim(out, parts[s], start, 1)
        return out

    q_all = lax.all_gather(queries, "dp", axis=0, tiled=True)

    def swap_dp(x, step):
        return lax.ppermute(x, "dp", [(i, i ^ step) for i in range(n_dp)])

    def beside(x, cols):
        if x.shape[1] <= cols:
            return jnp.concatenate(jnp.split(x, cols // x.shape[1], 0), 1)
        return jnp.concatenate(jnp.split(x, x.shape[1] // cols, 1), 0)

    def restored(x, cols):
        if cols <= x.shape[1]:
            return jnp.concatenate(jnp.split(x, x.shape[1] // cols, 1), 0)
        return jnp.concatenate(jnp.split(x, cols // x.shape[1], 0), 1)

    quarter = lax.rem(d, 4)
    odd, high = lax.rem(quarter, 2) == 1, quarter >= 2
    w1_rows, w2_rows = w1.shape[0] // 4, w2.shape[0] // 4
    piece = jnp.concatenate([
        lax.dynamic_slice_in_dim(w1, quarter * w1_rows, w1_rows),
        beside(lax.dynamic_slice_in_dim(w2, quarter * w2_rows, w2_rows), w1.shape[1]),
    ], 0)
    items = item_features.reshape(groups, quota, fg)
    sample_ids, piece = lax.optimization_barrier((sample_ids, piece))
    got = [shift(piece, s) for s in range(1, groups)]
    ids = sample_ids.reshape(groups, negs)
    far_rows = [
        corpus.at[at(ids, member + s)].get(mode="promise_in_bounds") for s in range(1, groups)
    ]
    far_rows, items, got = lax.optimization_barrier((far_rows, items, got))
    item_parts = [shift(at(items, member + s), s) for s in range(1, groups)]
    picked_parts = [shift(far_rows[s - 1], s) for s in range(1, groups)]
    own_rows = corpus.at[at(ids, member)].get(mode="promise_in_bounds")
    blocks = [jnp.concatenate([at(items, member), own_rows], 0)]
    for s in range(1, groups):
        blocks.append(jnp.concatenate([at(items, member + s), far_rows[s - 1]], 0))
    local = jnp.stack(blocks[:1] if groups == 2 else blocks)

    w1s, w2s = [w1], [w2]
    for p0 in got:
        p2 = swap_dp(p0, 2)
        p1, p3 = swap_dp(p0, 1), swap_dp(p2, 1)
        low = [jnp.where(odd, p1, p0), jnp.where(odd, p0, p1)]
        upp = [jnp.where(odd, p3, p2), jnp.where(odd, p2, p3)]
        placed = [jnp.where(high, u, l) for u, l in zip(upp, low)]
        placed += [jnp.where(high, l, u) for u, l in zip(upp, low)]
        w1s.append(jnp.concatenate([p[:w1_rows] for p in placed], 0))
        w2s.append(jnp.concatenate([restored(p[w1_rows:], emb) for p in placed], 0))

    feats = place_columns(
        blocks[:1]
        + [jnp.concatenate([a, b], 0) for a, b in zip(item_parts, picked_parts)]
    )

    embedded = jnp.zeros((rows, emb), F32)
    pre_own = None
    for s in range(groups):
        pre = mm(feats, w1s[s])
        hid = jnp.maximum(pre, 0.0).astype(BF16)
        if s == 0:
            pre_own, hid_own = pre, hid
        embedded = embedded + mm(hid, w2s[s])
    inverse = lax.rsqrt(jnp.mean(embedded * embedded, -1, keepdims=True) + 1e-06)
    normed = (embedded * inverse).astype(BF16)
    shift_own = lax.dynamic_slice_in_dim(sample_shift, member * negs, negs).astype(F32)
    bias = jnp.concatenate([jnp.zeros((quota,), F32), -shift_own])

    log_total, grad_hat, query_part, landed = score(
        groups, n_dp, local, q_all, normed, bias[:, None])
    log_total = log_total.reshape(-1)
    rest = place_columns(
        [jnp.concatenate(blocks[1:], 0)] + [landed[s - 1].reshape(-1, fg) for s in range(1, groups)]
    )

    query_own = lax.dynamic_slice_in_dim(queries, member * quota, quota).astype(F32)
    positive_own = normed[:quota].astype(F32)
    positive = scale * jnp.sum(query_own * positive_own, -1)
    query_loss = (
        lax.dynamic_slice_in_dim(log_total, d * query_rows + member * quota, quota) - positive
    )
    target = jnp.concatenate([query_own, jnp.zeros((negs, emb), F32)], 0)
    grad_normed = scale * (grad_hat - target)
    along = jnp.sum(grad_normed * embedded, -1, keepdims=True)
    grad_embed = (
        inverse * grad_normed - inverse**3 * embedded * along / emb
    ).astype(BF16)

    pre_rest = mm(rest, w1)
    hid_rest = jnp.maximum(pre_rest, 0.0).astype(BF16)
    back = jnp.concatenate(
        [grad_embed] + [shift(grad_embed, (groups - t) % groups) for t in range(1, groups)], 0
    )
    mask = jnp.concatenate([pre_own, pre_rest], 0) > 0
    grad_pre = jnp.where(mask, mm(back, w2.T), 0.0).astype(BF16)
    hid_all = jnp.concatenate([hid_own, hid_rest], 0)
    over_rows = (((0,), (0,)), ((), ()))
    grad_w2 = lax.dot_general(hid_all, back, over_rows, preferred_element_type=F32)
    feats_all = jnp.concatenate([feats, rest], 0)
    grad_w1 = lax.dot_general(feats_all, grad_pre, over_rows, preferred_element_type=F32)
    dp_bits = bits_of(n_dp)
    near, far = dp_bits[:1], dp_bits[:1:-1]
    along_first = [("dp", b) for b in near + dp_bits[1:2] + far]
    along_last = [("dp", b) for b in near + far + dp_bits[1:2]]
    query_order = (
        [("dp", near[0])]
        + [("group", b) for b in bits_of(groups)]
        + [("dp", b) for b in dp_bits[1:2] + far]
    )
    pad = -grad_w2.shape[0] % (16 * n_dp)
    padded = jnp.pad(grad_w2, ((0, pad), (0, 0)))
    xs = [
        grad_w1.reshape(2 * n_dp, -1, grad_w1.shape[1]),
        padded.reshape(n_dp, -1, emb),
        query_part.reshape(n_dp * groups, quota, emb),
    ]
    out_a, out_b, out_w2, query_sum = reduce_all(groups, n_dp, xs, [
        (0, 0, n_dp, along_last, True),
        (0, n_dp, n_dp, along_first, True),
        (1, 0, n_dp, along_first, True),
        (2, 0, n_dp * groups, query_order, False),
    ])
    grad_query = scale * (query_sum[0] - positive_own)
    grad_w1 = jnp.concatenate([out_a, out_b], 0).reshape(grad_w1.shape).astype(F32)
    grad_w2 = out_w2.reshape(padded.shape)[: grad_w2.shape[0]].astype(F32)
    return (query_loss, grad_query, grad_w1, grad_w2)


def solution(mesh):
    in_specs = (
        P("dp", None),
        P("dp", "group"),
        P("dp", "group"),
        P("dp"),
        P("dp"),
        P(None, "group"),
        P("group", None),
    )
    out_specs = (P(("dp", "group")), P(("dp", "group"), None), P(None, "group"), P("group", None))
    return jax.shard_map(
        per_device, mesh=mesh, in_specs=in_specs, out_specs=out_specs, check_vma=False
    )
```

profile of v0, /device:TPU:0, one launch (start us, length us, event | category | flops | bytes accessed | tf_op | source)
XLA Modules:
  0.0 227.1 jit_solution(15367139911487402381)
XLA Ops:
  9.7 3.0 %collective-permute-start = (bf16[576,512]{1,0:T(8,128)(2,1)}, bf16[576,512]{1,0:T(8,128)(2,1)}, u32[]{:S(2)}, u32[]{:S(2)}) collective-permute-start(bf16[576,512]{1,0:T(8,128)(2,1)} %maximum_maximum_fusion), channel_id=1, source_target_pairs={{0,1},{1,0},{2,3},{3,2},{4,5},{5,4},{6,7},{7,6},{8,9},{9,8},{10,11... | collective-permute-start | bytes 1769480 | tf_op jit(solution)/shard_map/ppermute | solution.py:275
  12.7 5.5 %gather_fusion = bf16[512,1024]{1,0:T(8,128)(2,1)S(1)} fusion(bf16[2048,1024]{1,0:T(8,128)(2,1)} %param.9, s32[1024]{0:T(1024)S(1)} %pad_clamp_fusion.1), kind=kCustom, calls=%fused_computation | custom fusion | bytes 2099200 | tf_op jit(solution)/shard_map/gather | solution.py:318
  18.2 8.1 %collective-permute-done = bf16[576,512]{1,0:T(8,128)(2,1)} collective-permute-done((bf16[576,512]{1,0:T(8,128)(2,1)}, bf16[576,512]{1,0:T(8,128)(2,1)}, u32[]{:S(2)}, u32[]{:S(2)}) %collective-permute-start) | collective-permute-done | bytes 589856 | tf_op jit(solution)/shard_map/ppermute | solution.py:275
  26.3 1.7 collective-permute-start.2
  28.0 1.5 collective-permute-start.3
  29.6 1.8 dynamic-slice_bitcast_fusion.1
  31.8 6.2 %gather_fusion.1 = bf16[512,1024]{1,0:T(8,128)(2,1)} fusion(bf16[2048,1024]{1,0:T(8,128)(2,1)} %param.9, s32[1024]{0:T(1024)S(1)} %pad_clamp_fusion), kind=kCustom, calls=%fused_computation.1 | custom fusion | bytes 2099200 | tf_op jit(solution)/shard_map/gather | solution.py:323
  40.1 16.3 %collective-permute-done.1 = bf16[128,1024]{1,0:T(8,128)(2,1)} collective-permute-done((bf16[128,1024]{1,0:T(8,128)(2,1)S(1)}, bf16[128,1024]{1,0:T(8,128)(2,1)}, u32[]{:S(2)}, u32[]{:S(2)}) %collective-permute-start.1) | collective-permute-done | bytes 262176 | tf_op jit(solution)/shard_map/ppermute | solution.py:275
  57.4 1.3 constant_dynamic-update-slice_fusion
  59.8 2.6 %maximum_convert_fusion.2 = (bf16[640,512]{1,0:T(8,128)(2,1)S(1)}, f32[640,512]{1,0:T(8,128)}) fusion(bf16[2048,512]{1,0:T(8,128)(2,1)S(1)} %copy-done, bf16[640,1024]{1,0:T(8,128)(2,1)S(1)} %get-tuple-element.33, bf16[640,1024]{1,0:T(8,128)(2,1)S(1)} %get-tuple-element.32), kind=kOutput, calls=%fused_computation.39 | convolution fusion | flops 1348075520 | bytes 6684672 | tf_op jit(solution)/shard_map/dot_general | solution.py:18
  62.4 1.2 fusion.46
  63.6 1.4 broadcast_select_fusion.6
  73.2 5.2 %multiply_reduce_fusion.1 = (f32[640]{0:T(1024)S(1)}, f32[640,256]{1,0:T(8,128)}) fusion(f32[640,256]{1,0:T(8,128)} %fusion.46, bf16[512,256]{1,0:T(8,128)(2,1)} %slice_dynamic-update-slice_fusion, bf16[512,512]{1,0:T(8,128)(2,1)} %slice.39, bf16[512,512]{1,0:T(8,128)(2,1)} %slice.38, bf16[512,512]{1,0:T(8,128)(2,1)} %slice.37, ...), kind=kOutput, calls=%fused_computation.48 | convolution fusion | flops 1524727168 | bytes 6294016 | tf_op jit(solution)/shard_map/dot_general | solution.py:18
  78.5 2.0 fusion.53
  80.4 1.9 copy.16.normed_t
  82.3 2.0 multiply_convert_fusion.normed
  84.3 1.6 copy-done.1
  88.8 44.0 %score.1 = (f32[16,256]{1,0:T(8,128)S(1)}, f32[640,256]{1,0:T(8,128)S(1)}, f32[4096,256]{1,0:T(8,128)}, bf16[1,1,640,1024]{3,2,1,0:T(8,128)(2,1)S(1)}) custom-call(bf16[1,640,1024]{2,1,0:T(8,128)(2,1)S(1)} %get-tuple-element.38.local, bf16[4096,256]{1,0:T(8,128)(2,1)S(1)} %copy-done.1, bf16[640,256]{1,0:T(8,128)(2,1)S(1)} %copy-done.2, ...), custom_call_target="tpu_custom_call" | custom-call | tf_op jit(solution)/shard_map/score/pallas_call | solution.py:110
  134.9 2.6 %maximum_convert_fusion = (bf16[640,512]{1,0:T(8,128)(2,1)S(1)}, f32[640,512]{1,0:T(8,128)}) fusion(bf16[2048,512]{1,0:T(8,128)(2,1)S(1)} %copy-done, bf16[640,1024]{1,0:T(8,128)(2,1)S(1)} %get-tuple-element.31, bf16[640,1024]{1,0:T(8,128)(2,1)S(1)} %get-tuple-element.30), kind=kOutput, calls=%fused_computation.37 | convolution fusion | flops 1348075520 | bytes 6684672 | tf_op jit(solution)/shard_map/dot_general | solution.py:18
  137.5 5.3 %collective-permute-done.6 = bf16[640,256]{1,0:T(8,128)(2,1)S(1)} collective-permute-done((bf16[640,256]{1,0:T(8,128)(2,1)S(1)}, bf16[640,256]{1,0:T(8,128)(2,1)S(1)}, u32[]{:S(2)}, u32[]{:S(2)}) %collective-permute-start.6) | collective-permute-done | bytes 327712 | tf_op jit(solution)/shard_map/ppermute | solution.py:275
  143.7 8.6 %fusion = f32[2048,512]{1,0:T(8,128)} fusion(bf16[640,1024]{1,0:T(8,128)(2,1)} %copy-done.12, bf16[640,1024]{1,0:T(8,128)(2,1)} %copy-done.11, bf16[640,1024]{1,0:T(8,128)(2,1)} %copy-done.10, bf16[640,1024]{1,0:T(8,128)(2,1)} %copy-done.9, bf16[512,256]{1,0:T(8,128)(2,1)S(1)} %copy-done.20, f32[640,512]{1,0:T(8,128)} %get-tuple-element.55, ...), kind=kOutput, calls=%fused_computation.2 | convolution fusion | flops 3044802560 | bytes 12976128 | tf_op jit(solution)/shard_map/dot_general | solution.py:389
  152.3 62.1 %reduce_all.1 = (bf16[16,64,512]{2,1,0:T(8,128)(2,1)S(1)}, bf16[16,64,512]{2,1,0:T(8,128)(2,1)S(1)}, bf16[16,32,256]{2,1,0:T(8,128)(2,1)S(1)}, f32[1,128,256]{2,1,0:T(8,128)S(1)}) custom-call(f32[32,64,512]{2,1,0:T(8,128)} %bitcast.40, f32[16,32,256]{2,1,0:T(8,128)S(1)} %bitcast.37, f32[32,128,256]{2,1,0:T(8,128)} %bitcast.39), custom_call_target="tpu_custom_call" | custom-call | tf_op jit(solution)/shard_map/reduce_all/pallas_call | solution.py:247
  214.6 2.7 %bitcast_convert_fusion = f32[2048,512]{1,0:T(8,128)} fusion(bf16[32,64,512]{2,1,0:T(8,128)(2,1)S(1)} %pad_maximum_fusion.1), kind=kLoop, calls=%fused_computation.27 | loop fusion | flops 1048576 | bytes 6291456 | tf_op jit(solution)/shard_map/convert_element_type | solution.py:413
  218.2 1.5 fusion.33
  (90 shorter events, 22.7 us)
Async XLA Ops:
  7.2 1.6 copy-start
  7.2 5.5 %copy-start.21 = (s32[1024]{0:T(1024)S(1)}, s32[1024]{0:T(1024)}, u32[]{:S(2)}) copy-start(s32[1024]{0:T(1024)} %param.10) | copy-start | bytes 12292
  7.2 77.1 %all-gather.2.cloned.1.call-start = ((), (), s32[]{:S(2)}) async-start(), calls=%async_computation | async-start | bytes 2228224 | tf_op jit(solution)/shard_map/all_gather | solution.py:291
  9.7 16.6 %collective-permute-start = (bf16[576,512]{1,0:T(8,128)(2,1)}, bf16[576,512]{1,0:T(8,128)(2,1)}, u32[]{:S(2)}, u32[]{:S(2)}) collective-permute-start(bf16[576,512]{1,0:T(8,128)(2,1)} %maximum_maximum_fusion), channel_id=1, source_target_pairs={{0,1},{1,0},{2,3},{3,2},{4,5},{5,4},{6,7},{7,6},{8,9},{9,8},{10,11... | collective-permute-start | bytes 1769480 | tf_op jit(solution)/shard_map/ppermute | solution.py:275
  18.2 19.9 %copy-start.6 = (bf16[512,1024]{1,0:T(8,128)(2,1)}, bf16[512,1024]{1,0:T(8,128)(2,1)S(1)}, u32[]{:S(2)}) copy-start(bf16[512,1024]{1,0:T(8,128)(2,1)S(1)} %gather_fusion) | copy-start | bytes 3145732
  26.3 31.1 %collective-permute-start.2 = (bf16[512,1024]{1,0:T(8,128)(2,1)S(1)}, bf16[512,1024]{1,0:T(8,128)(2,1)}, u32[]{:S(2)}, u32[]{:S(2)}) collective-permute-start(bf16[512,1024]{1,0:T(8,128)(2,1)S(1)} %gather_fusion), channel_id=1, source_target_pairs={{0,1},{1,0},{2,3},{3,2},{4,5},{5,4},{6,7},{7,6},{8,9},{9,8},{10,11... | collective-permute-start | bytes 3145736 | tf_op jit(solution)/shard_map/ppermute | solution.py:275
  28.0 29.3 %collective-permute-start.3 = (bf16[576,512]{1,0:T(8,128)(2,1)}, bf16[576,512]{1,0:T(8,128)(2,1)}, u32[]{:S(2)}, u32[]{:S(2)}) collective-permute-start(bf16[576,512]{1,0:T(8,128)(2,1)} %collective-permute-done), channel_id=1, source_target_pairs={{0,4},{2,6},{4,0},{6,2},{8,12},{10,14},{12,8},{14,10},{16,20},{18,... | collective-permute-start | bytes 1769480 | tf_op jit(solution)/shard_map/ppermute | solution.py:294
  31.3 6.7 %copy-start.13 = (bf16[128,1024]{1,0:T(8,128)(2,1)}, bf16[128,1024]{1,0:T(8,128)(2,1)S(1)}, u32[]{:S(2)}) copy-start(bf16[128,1024]{1,0:T(8,128)(2,1)S(1)} %get-tuple-element.40) | copy-start | bytes 786436
  31.3 25.0 %collective-permute-start.1 = (bf16[128,1024]{1,0:T(8,128)(2,1)S(1)}, bf16[128,1024]{1,0:T(8,128)(2,1)}, u32[]{:S(2)}, u32[]{:S(2)}) collective-permute-start(bf16[128,1024]{1,0:T(8,128)(2,1)S(1)} %get-tuple-element.40), channel_id=1, source_target_pairs={{0,1},{1,0},{2,3},{3,2},{4,5},{5,4},{6,7},{7,6},{8,9},{9,8},{10,11... | collective-permute-start | bytes 786440 | tf_op jit(solution)/shard_map/ppermute | solution.py:275
  31.8 6.2 %copy-start.22 = (bf16[1024]{0:T(1024)(128)(2,1)S(1)}, bf16[1024]{0:T(1024)(128)(2,1)}, u32[]{:S(2)}) copy-start(bf16[1024]{0:T(1024)(128)(2,1)} %param.11) | copy-start | bytes 6148
  39.0 19.7 %copy-start.8 = (bf16[512,1024]{1,0:T(8,128)(2,1)S(1)}, bf16[512,1024]{1,0:T(8,128)(2,1)}, u32[]{:S(2)}) copy-start(bf16[512,1024]{1,0:T(8,128)(2,1)} %gather_fusion.1) | copy-start | bytes 3145732
  39.0 19.7 %copy-start.15 = (bf16[128,1024]{1,0:T(8,128)(2,1)S(1)}, bf16[128,1024]{1,0:T(8,128)(2,1)}, u32[]{:S(2)}) copy-start(bf16[128,1024]{1,0:T(8,128)(2,1)} %get-tuple-element.39) | copy-start | bytes 786436
  40.0 23.6 %collective-permute-start.5 = (bf16[576,512]{1,0:T(8,128)(2,1)}, bf16[576,512]{1,0:T(8,128)(2,1)S(1)}, u32[]{:S(2)}, u32[]{:S(2)}) collective-permute-start(bf16[576,512]{1,0:T(8,128)(2,1)} %collective-permute-done), channel_id=1, source_target_pairs={{0,2},{2,0},{4,6},{6,4},{8,10},{10,8},{12,14},{14,12},{16,18},{18,... | collective-permute-start | bytes 1769480 | tf_op jit(solution)/shard_map/ppermute | solution.py:294
  57.3 6.2 %collective-permute-start.4 = (bf16[576,512]{1,0:T(8,128)(2,1)}, bf16[576,512]{1,0:T(8,128)(2,1)S(1)}, u32[]{:S(2)}, u32[]{:S(2)}) collective-permute-start(bf16[576,512]{1,0:T(8,128)(2,1)} %collective-permute-done.3), channel_id=1, source_target_pairs={{0,2},{2,0},{4,6},{6,4},{8,10},{10,8},{12,14},{14,12},{16,18},{18,... | collective-permute-start | bytes 1769480 | tf_op jit(solution)/shard_map/ppermute | solution.py:294
  59.7 2.7 %copy-start.9 = (bf16[640,1024]{1,0:T(8,128)(2,1)}, bf16[640,1024]{1,0:T(8,128)(2,1)S(1)}, u32[]{:S(2)}) copy-start(bf16[640,1024]{1,0:T(8,128)(2,1)S(1)} %get-tuple-element.32) | copy-start | bytes 3932164
  59.7 2.7 %copy-start.10 = (bf16[640,1024]{1,0:T(8,128)(2,1)}, bf16[640,1024]{1,0:T(8,128)(2,1)S(1)}, u32[]{:S(2)}) copy-start(bf16[640,1024]{1,0:T(8,128)(2,1)S(1)} %get-tuple-element.33) | copy-start | bytes 3932164
  59.7 2.7 %copy-start.19 = (bf16[512,256]{1,0:T(8,128)(2,1)S(1)}, bf16[512,256]{1,0:T(8,128)(2,1)}, u32[]{:S(2)}) copy-start(bf16[512,256]{1,0:T(8,128)(2,1)} %param.13) | copy-start | bytes 786436
  84.3 1.6 copy-start.1
  88.8 44.1 %copy-start.5 = (f32[640,256]{1,0:T(8,128)S(1)}, f32[640,256]{1,0:T(8,128)}, u32[]{:S(2)}) copy-start(f32[640,256]{1,0:T(8,128)} %get-tuple-element.53) | copy-start | bytes 1966084
  133.4 9.4 %collective-permute-start.6 = (bf16[640,256]{1,0:T(8,128)(2,1)S(1)}, bf16[640,256]{1,0:T(8,128)(2,1)S(1)}, u32[]{:S(2)}, u32[]{:S(2)}) collective-permute-start(bf16[640,256]{1,0:T(8,128)(2,1)S(1)} %subtract_convert_fusion), channel_id=1, source_target_pairs={{0,1},{1,0},{2,3},{3,2},{4,5},{5,4},{6,7},{7,6},{8,9},{9,8},{10,11... | collective-permute-start | bytes 983048 | tf_op jit(solution)/shard_map/ppermute | solution.py:275
  134.8 2.7 %copy-start.11 = (bf16[640,1024]{1,0:T(8,128)(2,1)}, bf16[640,1024]{1,0:T(8,128)(2,1)S(1)}, u32[]{:S(2)}) copy-start(bf16[640,1024]{1,0:T(8,128)(2,1)S(1)} %get-tuple-element.30) | copy-start | bytes 3932164
  134.8 2.7 %copy-start.12 = (bf16[640,1024]{1,0:T(8,128)(2,1)}, bf16[640,1024]{1,0:T(8,128)(2,1)S(1)}, u32[]{:S(2)}) copy-start(bf16[640,1024]{1,0:T(8,128)(2,1)S(1)} %get-tuple-element.31) | copy-start | bytes 3932164
  134.9 7.9 %copy-start.17 = (bf16[640,512]{1,0:T(8,128)(2,1)S(1)}, bf16[640,512]{1,0:T(8,128)(2,1)}, u32[]{:S(2)}) copy-start(bf16[640,512]{1,0:T(8,128)(2,1)} %copy-done.16) | copy-start | bytes 1966084
  214.6 3.6 %copy-start.18 = (bf16[256,256]{1,0:T(8,128)(2,1)S(1)}, bf16[256,256]{1,0:T(8,128)(2,1)}, u32[]{:S(2)}) copy-start(bf16[256,256]{1,0:T(8,128)(2,1)} %param.7) | copy-start | bytes 393220
  (7 other events, 7.5 us)
Sparse Core Ops, SparseCore 0:
  29.7 41.4 all-gather.1
where the time goes:
time: 228 us; the launch traced here: 227 us
  Pallas kernels  106 us (46%)
  local copies, waits for them, and re-layouts  33.4 us (15%)
  waiting for transfers between devices  29.7 us (13%)
  matrix products  20.8 us (9%)
  other arithmetic  15.4 us (7%)
  between operations  14.3 us (6%)
  starting transfers between devices  7.46 us (3%)
    pallas_call x1, Pallas kernels, reduce_all(): pl.pallas_call(functools.partial(reduce_kernel, plans, len(xs), peers), o...  62.1 us
    pallas_call x1, Pallas kernels, score(): pl.pallas_call(functools.partial(score_kernel, groups, n_dp), out_shape=(...  44 us
    ppermute x4, waiting for transfers between devices, shift(): lax.ppermute(x, 'group', [(i, (i + s) % groups) for i in range(groups)])  29.7 us
    dot_general x4, matrix products, mm(): return jnp.dot(a, b, preferred_element_type=F32)  11.7 us
    unnamed x55, local copies, waits for them, and re-layouts  11 us
    dot_general x1, matrix products, per_device(): lax.dot_general(feats_all, grad_pre, over_rows, preferred_element_type=F32)  8.59 us
    gather x1, local copies, waits for them, and re-layouts, per_device(): own_rows = corpus.at[at(ids, member)].get(mode='promise_in_bounds')  6.21 us
    ppermute x4, starting transfers between devices, shift(): lax.ppermute(x, 'group', [(i, (i + s) % groups) for i in range(groups)])  5.79 us
  transfers between devices with their start and end apart: 8, of which 3 were waited for; matrix products, arithmetic and copies ran while one was open for 20% of the time, Pallas kernels for 0%

commit v1 on v0

--- a/solution.py
+++ b/solution.py
@@ -259,11 +259,602 @@
     )(*xs)
 
 
+def nt(a, b):
+    return lax.dot_general(a, b, (((1,), (1,)), ((), ())), preferred_element_type=F32)
+
+
+def tn(a, b):
+    return lax.dot_general(a, b, (((0,), (0,)), ((), ())), preferred_element_type=F32)
+
+
+def loop(n, body):
+    def step(i, carry):
+        body(i)
+        return carry
+
+    lax.fori_loop(0, n, step, 0)
+
+
+def weights_of(order):
+    return {axis_step: 1 << (len(order) - 1 - k) for k, axis_step in enumerate(order)}
+
+
+class Plan:
+    def __init__(self, n_dp, queries, items, corpus, w1, w2):
+        self.n_dp = n_dp
+        self.query_rows, self.emb = queries.shape
+        self.quota = self.query_rows // 2
+        self.fg = items.shape[1]
+        self.slab = corpus.shape[0]
+        self.feats, self.hg = w1.shape
+        bits = bits_of(n_dp)
+        core, x, z = bits[0], bits[1], bits[2:]
+        dp = lambda steps: [("dp", s) for s in steps]
+        y = [("group", 1)]
+        self.gather_order = [x] + z[::-1] + [core]
+        self.q_order = dp([core, x]) + y + dp(z)
+        self.w_orders = [
+            dp([core]) + y + dp([x]) + dp(z),
+            dp([core, x]) + y + dp(z),
+            dp([core]) + dp(z) + dp([x]) + y,
+        ]
+        self.w2_order = self.w_orders[1]
+        self.bits = bits
+
+
+PART_ROWS = (0, 48, 96, 128)
+CH = 128
+
+
+def fused_kernel(pn, rows, queries, items, corpus, meta_in, w1, w2,
+                 loss_ref, gq_ref, gw1_ref, gw2_ref,
+                 big, q_all, w1v, w2v, mine, peer, far, hot, meta, pre, hid, emb, nrm, nrms, nrm_t,
+                 bias, hat, logits, qpt, stats, arrived, total_ref, fac, featt, gp, ge,
+                 recv, ag, qsend, qrecv, acc2, send2, recv2, ag2, lsem, ssem, rsem):
+    n_dp, width, fg, hg, slab = pn.n_dp, pn.query_rows, pn.fg, pn.hg, pn.slab
+    quota, e_dim = pn.quota, pn.emb
+    negs = rows - quota
+    chunks = negs // CH
+    scale = e_dim ** (-0.5)
+    m = lax.axis_index("group")
+    d = lax.axis_index("dp")
+    other = 1 - m
+    ypeer = partner("group", 1)[1]
+    core, xbit = pn.bits[0], pn.bits[1]
+    rounds = [("dp", s) for s in pn.bits] + [("group", 1)]
+    count = iter(range(1000))
+    lcount = iter(range(100))
+
+    def bit(step):
+        return lax.rem(lax.div(d, step), 2)
+
+    def remote(src, dst, to, k=None):
+        k = next(count) if k is None else k
+        return pltpu.make_async_remote_copy(
+            src_ref=src, dst_ref=dst, send_sem=ssem.at[k], recv_sem=rsem.at[k],
+            device_id=to, device_id_type=MESH)
+
+    def local(src, dst):
+        copy = pltpu.make_async_copy(src, dst, lsem.at[next(lcount)])
+        copy.start()
+        return copy
+
+    gw = {s: 1 << k for k, s in enumerate(pn.gather_order)}
+    pos = sum(bit(s) * gw[s] for s in pn.bits)
+    tiles = n_dp
+
+    c_q = local(queries, q_all.at[pos])
+    c_meta = local(meta_in, meta)
+    c_slab = [local(corpus.at[:, n * 256 : (n + 1) * 256], big.at[n * slab : (n + 1) * slab])
+              for n in range(fg // 256)]
+    c_mine = local(items.at[pl.ds(pl.multiple_of(m * quota, quota), quota)], mine.at[0:quota])
+    c_w1 = local(w1, w1v.at[0])
+    c_w2 = local(w2, w2v.at[0])
+    greet([partner(a, b)[1] for a, b in rounds])
+
+    e = bit(core) * 2 + bit(xbit)
+    q1, q2 = w1.shape[0] // 4, w2.shape[0] // 4
+
+    def span(n, base, size):
+        return pl.ds(pl.multiple_of(base * n, n), n * size)
+
+    wy = [remote(w1.at[span(q1, e, 1)], w1v.at[1, span(q1, e, 1)], ypeer),
+          remote(w2.at[span(q2, e, 1)], w2v.at[1, span(q2, e, 1)], ypeer)]
+    for c in wy:
+        c.start()
+    item_send = remote(items.at[pl.ds(pl.multiple_of(other * quota, quota), quota)],
+                       peer.at[0:quota], ypeer)
+    item_send.start()
+    c_q.wait()
+    q_steps = pn.gather_order
+
+    def q_gather(k):
+        size = 1 << k
+        base = lax.div(pos, size) * size
+        view = q_all.at[pl.ds(base, size)]
+        c = remote(view, view, partner("dp", q_steps[k])[1])
+        c.start()
+        return c
+
+    qg = q_gather(0)
+    k_far = [next(count) for _ in range(chunks)][0]
+
+    def rows_at(k):
+        return pl.ds(pl.multiple_of(quota + k * CH, CH), CH)
+
+    def far_copy(k):
+        return remote(far.at[pl.ds(pl.multiple_of(k * CH, CH), CH)], peer.at[rows_at(k)],
+                      ypeer, k_far + k)
+
+    def column(r):
+        return jnp.broadcast_to(meta[pl.ds(r, 1), :], (8, CH)).T[:, :1]
+
+    def pick(who, k, dst, at):
+        ids = column(who * chunks + k)
+        where = lax.broadcasted_iota(jnp.int32, (CH, slab), 1).astype(F32)
+        hot[...] = jnp.where(ids == where, 1.0, 0.0).astype(BF16)
+        for n in range(fg // 256):
+            dst[at, n * 256 : (n + 1) * 256] = mm(
+                hot[...], big[n * slab : (n + 1) * slab, :]).astype(BF16)
+
+    c_meta.wait()
+    for c in c_slab:
+        c.wait()
+
+    def pick_far(k):
+        pick(other, k, far, pl.ds(pl.multiple_of(k * CH, CH), CH))
+        far_copy(k).start()
+
+    loop(chunks, pick_far)
+    qg.wait()
+    qg = q_gather(1)
+    loop(chunks, lambda k: pick(m, k, mine, rows_at(k)))
+    bias[0:quota, :] = jnp.zeros((quota, width), F32)
+
+    def put_bias(k):
+        bias[rows_at(k), :] = jnp.broadcast_to(
+            -column(2 * chunks + m * chunks + k), (CH, width))
+
+    loop(chunks, put_bias)
+    c_mine.wait()
+    c_w1.wait()
+    c_w2.wait()
+
+    nj = hg // 256
+
+    def tower_add(r0, r1, feat, half, c, first):
+        for j in range(nj):
+            part = mm(feat[r0:r1, :], w1v[c, pl.ds(pl.multiple_of(half * fg, fg), fg),
+                                         j * 256 : (j + 1) * 256])
+            if first:
+                pre[c * nj + j, r0:r1, :] = part
+            else:
+                pre[c * nj + j, r0:r1, :] += part
+
+    tower_add(0, rows, mine, m, 0, True)
+    for c in wy:
+        c.wait()
+    pair = lax.div(e, 2) * 2
+    wx = [remote(w1v.at[1, span(q1, e, 1)], w1v.at[1, span(q1, e, 1)], partner("dp", xbit)[1]),
+          remote(w2v.at[1, span(q2, e, 1)], w2v.at[1, span(q2, e, 1)], partner("dp", xbit)[1])]
+    for c in wx:
+        c.start()
+    for k in range(2, len(q_steps) - 1):
+        qg.wait()
+        qg = q_gather(k)
+
+    def turn(src, half, n):
+        at = pl.multiple_of(n * 256, 256)
+        featt[pl.ds(pl.multiple_of(half * fg + at, 256), 256), :] = src[:, pl.ds(at, 256)].T
+
+    loop(fg // 256, lambda n: turn(mine, m, n))
+    for c in wx:
+        c.wait()
+    wc = [remote(w1v.at[1, span(q1, pair, 2)], w1v.at[1, span(q1, pair, 2)], partner("dp", core)[1]),
+          remote(w2v.at[1, span(q2, pair, 2)], w2v.at[1, span(q2, pair, 2)], partner("dp", core)[1])]
+    for c in wc:
+        c.start()
+    qg.wait()
+    qg = q_gather(len(q_steps) - 1)
+    for c in wc:
+        c.wait()
+    tower_add(0, rows, mine, m, 1, True)
+
+    def finish_tower(r0, r1):
+        loop(2, lambda c: tower_add(r0, r1, peer, other, c, False))
+        emb[r0:r1, :] = jnp.zeros((r1 - r0, e_dim), F32)
+
+        def second_layer(c):
+            for j in range(nj):
+                h = jnp.maximum(pre[c * nj + j, r0:r1, :], 0.0).astype(BF16)
+                hid[c * nj + j, r0:r1, :] = h
+                emb[r0:r1, :] += mm(h, w2v[c, j * 256 : (j + 1) * 256, :])
+
+        loop(2, second_layer)
+        em = emb[r0:r1, :]
+        inv = lax.rsqrt(jnp.mean(em * em, -1, keepdims=True) + 1e-06)
+        no = (em * inv).astype(BF16)
+        nrm[r0:r1, :] = no
+        nrms[r0:r1, :] = (no.astype(F32) * scale).astype(BF16)
+        nrm_t[:, r0:r1] = no.astype(F32).T.astype(BF16)
+
+    oq = weights_of(pn.q_order)
+    gq = oq[("group", 1)]
+
+    def shard_of(i):
+        return sum(lax.rem(lax.div(i, gw[s]), 2) * oq[("dp", s)] for s in pn.bits)
+
+    ra = rows - CH
+    half_q = width // 2
+
+    def score_a(i):
+        block = nt(nrms[0:ra, :], q_all[i]) + bias[0:ra, :]
+        logits[i, 0:ra, :] = block
+        top = jnp.max(block, 0, keepdims=True)
+        p = jnp.exp(block - top)
+        stats[0, 0, pl.ds(i, 1), :] = top
+        stats[0, 1, pl.ds(i, 1), :] = jnp.sum(p, 0, keepdims=True)
+        part = mm(nrm_t[:, 0:ra], p.astype(BF16))
+        j = shard_of(i)
+        for g in range(2):
+            qpt[j + g * gq] = part[:, g * half_q : (g + 1) * half_q]
+
+    def score_b(i):
+        block = nt(nrms[ra:rows, :], q_all[i]) + bias[ra:rows, :]
+        logits[i, ra:rows, :] = block
+        before = stats[0, 0, pl.ds(i, 1), :]
+        top = jnp.maximum(before, jnp.max(block, 0, keepdims=True))
+        shrink = jnp.exp(before - top)
+        p = jnp.exp(block - top)
+        stats[0, 0, pl.ds(i, 1), :] = top
+        stats[0, 1, pl.ds(i, 1), :] = (
+            stats[0, 1, pl.ds(i, 1), :] * shrink + jnp.sum(p, 0, keepdims=True))
+        part = mm(nrm_t[:, ra:rows], p.astype(BF16))
+        j = shard_of(i)
+        for g in range(2):
+            cut = slice(g * half_q, (g + 1) * half_q)
+            qpt[j + g * gq] = qpt[j + g * gq] * shrink[:, cut] + part[:, cut]
+
+    item_send.wait()
+    loop(chunks - 1, lambda k: far_copy(k).wait())
+    finish_tower(0, ra)
+    qg.wait()
+    loop(tiles, score_a)
+    far_copy(chunks - 1).wait()
+    finish_tower(ra, rows)
+    loop(tiles, score_b)
+
+    for r, (axis, step) in enumerate(rounds):
+        copy = remote(stats.at[r], arrived.at[r], partner(axis, step)[1])
+        copy.start()
+        if r == 0:
+            loop(fg // 256, lambda n: turn(peer, other, n))
+        copy.wait()
+        m0, s0, m1, s1 = stats[r, 0], stats[r, 1], arrived[r, 0], arrived[r, 1]
+        top = jnp.maximum(m0, m1)
+        stats[r + 1, 0] = top
+        stats[r + 1, 1] = s0 * jnp.exp(m0 - top) + s1 * jnp.exp(m1 - top)
+    last = len(rounds)
+    total_ref[...] = stats[last, 0] + jnp.log(stats[last, 1])
+    fac[...] = jnp.exp(stats[0, 0] - total_ref[...])
+
+    class Chain:
+        def __init__(self, order, put, add, send_at, recv_at):
+            self.order, self.put, self.add = order, put, add
+            self.send_at, self.recv_at = send_at, recv_at
+            self.n = 1 << len(order)
+            self.base = 0
+
+        def begin(self, r):
+            half = self.n >> (r + 1)
+            at0 = self.n - 2 * half
+            b, to = partner(*self.order[r])
+            if r > 0:
+                base = self.base
+                loop(half, lambda j: self.put(at0 + j, base + (1 - b) * half + j))
+            self.copy = remote(self.send_at(at0, half), self.recv_at(at0, half), to)
+            self.copy.start()
+
+        def finish(self, r):
+            half = self.n >> (r + 1)
+            at0 = self.n - 2 * half
+            b, _ = partner(*self.order[r])
+            self.copy.wait()
+            if r > 0:
+                self.base = self.base + b * half
+            base = self.base
+            loop(half, lambda j: self.add(base + j, at0 + j))
+
+        def step(self, r):
+            if r > 0:
+                self.finish(r - 1)
+            if r < len(self.order):
+                self.begin(r)
+
+    cb = bit(core)
+    own16 = cb * n_dp
+
+    def q_put(slot, a):
+        qsend[slot] = qpt[own16 + a].astype(BF16)
+
+    def q_add(a, slot):
+        qpt[own16 + a] = qpt[own16 + a] + qrecv[slot].astype(F32)
+
+    q_chain = Chain(pn.q_order, q_put, q_add,
+                    lambda a, n: qsend.at[pl.ds(a, n)], lambda a, n: qrecv.at[pl.ds(a, n)])
+
+    def scale_q(i):
+        f = fac[pl.ds(i, 1), :]
+        j = shard_of(i)
+        for g in range(2):
+            qpt[j + g * gq] = qpt[j + g * gq] * f[:, g * half_q : (g + 1) * half_q]
+
+    loop(tiles, scale_q)
+    loop(n_dp, lambda j: q_put(j, (1 - 2 * cb) * n_dp + j))
+    q_chain.begin(0)
+
+    hat[...] = jnp.zeros_like(hat)
+
+    def second(i):
+        p = jnp.exp(logits[i] - total_ref[pl.ds(i, 1), :]).astype(BF16)
+        hat[...] += mm(p, q_all[i])
+
+    loop(tiles, second)
+    q_chain.step(1)
+
+    q_own = q_all[pos, pl.ds(pl.multiple_of(m * quota, quota), quota), :].astype(F32)
+    positive = nrm[0:quota, :].astype(F32)
+    mine_total = total_ref[pl.ds(pos, 1), :]
+    mine_total = jnp.where(m == 0, mine_total[:, :half_q], mine_total[:, half_q:])
+    loss_ref[...] = mine_total - scale * jnp.sum((q_own * positive).T, 0, keepdims=True)
+
+    hat[0:quota, :] = hat[0:quota, :] - q_own
+    em = emb[...]
+    inv = lax.rsqrt(jnp.mean(em * em, -1, keepdims=True) + 1e-06)
+    gn = scale * hat[...]
+    along = jnp.sum(gn * em, -1, keepdims=True)
+    ge[...] = (inv * gn - inv**3 * em * along / e_dim).astype(BF16)
+
+    def back(c):
+        for j in range(nj):
+            g = nt(ge[...], w2v[c, j * 256 : (j + 1) * 256, :])
+            gp[c * nj + j] = jnp.where(pre[c * nj + j] > 0, g, 0.0).astype(BF16)
+
+    loop(2, back)
+
+    half_f = pn.feats // 2
+    per_core = n_dp // 2
+    n_all = 2 * n_dp
+
+    def place(fb, g, order):
+        w = weights_of(order)[("group", 1)]
+        return (fb // w) * 2 * w + g * w + fb % w
+
+    def group_of(c):
+        return m if c == 0 else other
+
+    def w1_half(cbit, sink):
+        for c in range(2):
+            for t in range(nj):
+                r = mm(featt[pl.ds(pl.multiple_of(cbit * half_f, half_f), half_f), :], gp[c * nj + t])
+                for fb in range(per_core):
+                    for p, order in enumerate(pn.w_orders):
+                        p0, p1 = PART_ROWS[p], PART_ROWS[p + 1]
+                        sink(p, place(fb, group_of(c), order), t,
+                             r[fb * CH + p0 : fb * CH + p1, :])
+
+    def slot_at(p, slot, n):
+        p0, p1 = PART_ROWS[p], PART_ROWS[p + 1]
+        pr = (p1 - p0) * nj
+        return pl.ds(pl.multiple_of((n_all - 1) * nj * p0 + slot * pr, 16), n * pr)
+
+    def sink_send(p, j, t, v):
+        pr = PART_ROWS[p + 1] - PART_ROWS[p]
+        at = (n_all - 1) * nj * PART_ROWS[p] + j * (nj * pr) + t * pr
+        big[pl.ds(pl.multiple_of(at, 16), pr), :] = v.astype(BF16)
+
+    def sink_acc(p, j, t, v):
+        p0, p1 = PART_ROWS[p], PART_ROWS[p + 1]
+        logits[j, t * CH + p0 : t * CH + p1, :] = v
+
+    def w_chain(p):
+        p0, p1 = PART_ROWS[p], PART_ROWS[p + 1]
+        pr = p1 - p0
+
+        def put(slot, a):
+            for t in range(nj):
+                sink_send(p, slot, t, logits[a, t * CH + p0 : t * CH + p1, :])
+
+        def add(a, slot):
+            at = (n_all - 1) * nj * p0 + slot * (nj * pr)
+            for t in range(nj):
+                cut = slice(t * CH + p0, t * CH + p1)
+                logits[a, cut, :] = logits[a, cut, :] + recv[
+                    pl.ds(pl.multiple_of(at + t * pr, 16), pr), :].astype(F32)
+
+        return Chain(pn.w_orders[p], put, add,
+                     lambda s, n: big.at[slot_at(p, s, n)], lambda s, n: recv.at[slot_at(p, s, n)])
+
+    h2 = 256 // per_core
+
+    def w2_half(cbit, sink):
+        for c in range(2):
+            r = tn(hid[c * nj + cbit], ge[...])
+            for fb in range(per_core):
+                sink(place(fb, group_of(c), pn.w2_order), r[fb * h2 : (fb + 1) * h2, :])
+
+    def w2_send(j, v):
+        send2[j] = v.astype(BF16)
+
+    def w2_acc(j, v):
+        acc2[j] = v
+
+    def w2_put(slot, a):
+        send2[slot] = acc2[a].astype(BF16)
+
+    def w2_add(a, slot):
+        acc2[a] = acc2[a] + recv2[slot].astype(F32)
+
+    chains = [w_chain(p) for p in range(len(pn.w_orders))]
+    w2_chain = Chain(pn.w2_order, w2_put, w2_add,
+                     lambda a, n: send2.at[pl.ds(a, n)], lambda a, n: recv2.at[pl.ds(a, n)])
+    w1_half(1 - cb, sink_send)
+    for ch in chains:
+        ch.begin(0)
+    w2_half(1 - cb, w2_send)
+    w2_chain.begin(0)
+    q_chain.step(2)
+    w1_half(cb, sink_acc)
+    w2_half(cb, w2_acc)
+    every = chains + [w2_chain]
+    steps = len(pn.w2_order)
+    for r in range(1, steps + 1):
+        for ch in every:
+            ch.step(r)
+        if r + 2 <= steps:
+            q_chain.step(r + 2)
+
+    q_sum = qpt[own16 + q_chain.base]
+    gq_ref[...] = scale * (q_sum.T - positive)
+
+    def block_of(ch):
+        w = weights_of(ch.order)[("group", 1)]
+        return cb * per_core + lax.div(ch.base, 2 * w) * w + lax.rem(ch.base, w)
+
+    def ag_at(p, fb, n):
+        p0, p1 = PART_ROWS[p], PART_ROWS[p + 1]
+        pr = (p1 - p0) * nj
+        return pl.ds(pl.multiple_of(n_dp * nj * p0 + fb * pr, 16), n * pr)
+
+    views = []
+    for p, ch in enumerate(chains):
+        p0, p1 = PART_ROWS[p], PART_ROWS[p + 1]
+        pr = p1 - p0
+        fb = block_of(ch)
+        for t in range(nj):
+            at = n_dp * nj * p0 + fb * (nj * pr) + t * pr
+            ag[pl.ds(pl.multiple_of(at, 16), pr), :] = logits[
+                ch.base, t * CH + p0 : t * CH + p1, :].astype(BF16)
+        views.append((ch, fb, functools.partial(lambda p, b, n: ag.at[ag_at(p, b, n)], p)))
+    fb2 = block_of(w2_chain)
+    ag2[fb2] = acc2[w2_chain.base].astype(BF16)
+    views.append((w2_chain, fb2, lambda b, n: ag2.at[pl.ds(b, n)]))
+    live = [None] * len(views)
+    for k in range(len(pn.bits)):
+        for i, (ch, fb, view) in enumerate(views):
+            if live[i] is not None:
+                live[i].wait()
+            back_order = [a for a in ch.order if a[0] == "dp"][::-1]
+            size = 1 << k
+            v = view(lax.div(fb, size) * size, size)
+            live[i] = remote(v, v, partner(*back_order[k])[1])
+            live[i].start()
+    for c in live:
+        c.wait()
+
+    for p in range(len(chains)):
+        p0, p1 = PART_ROWS[p], PART_ROWS[p + 1]
+        pr = p1 - p0
+
+        def out_rows(fb):
+            for t in range(nj):
+                at = n_dp * nj * p0 + fb * (nj * pr) + t * pr
+                gw1_ref[pl.ds(pl.multiple_of(fb * CH + p0, 16), pr), t * 256 : (t + 1) * 256] = ag[
+                    pl.ds(pl.multiple_of(at, 16), pr), :].astype(F32)
+
+        loop(n_dp, out_rows)
+    gw2_ref[...] = ag2[...].reshape(gw2_ref.shape).astype(F32)
+
+
+def fused(n_dp, queries, items, corpus, sample_ids, sample_shift, w1, w2):
+    pn = Plan(n_dp, queries, items, corpus, w1, w2)
+    width, emb = queries.shape
+    negs = sample_ids.shape[0] // 2
+    rows = pn.quota + negs
+    fg, feats, hg = pn.fg, pn.feats, pn.hg
+    nj = hg // 256
+    n_all = 2 * n_dp
+    rounds = n_all.bit_length() - 1
+    meta = jnp.concatenate([sample_ids.astype(F32), sample_shift.astype(F32)]).reshape(-1, CH)
+    half = feats // 2
+    sends = (n_all - 1) * nj * CH
+    big = -(-max(sends, (fg // 256) * pn.slab) // 16) * 16
+    hp = hg // n_dp
+    n_sem = 80
+    S = pltpu.VMEM
+    loss, gq, gw1, gw2 = pl.pallas_call(
+        functools.partial(fused_kernel, pn, rows),
+        out_shape=(
+            jax.ShapeDtypeStruct((1, pn.quota), F32),
+            jax.ShapeDtypeStruct((pn.quota, emb), F32),
+            jax.ShapeDtypeStruct((feats, hg), F32),
+            jax.ShapeDtypeStruct((hg, emb), F32),
+        ),
+        in_specs=[ANY] * 6,
+        out_specs=(VMEM,) * 4,
+        scratch_shapes=[
+            S((big, 256), BF16),
+            S((n_dp, width, emb), BF16),
+            S((2, feats, hg), BF16),
+            S((2, hg, emb), BF16),
+            S((rows, fg), BF16),
+            S((rows, fg), BF16),
+            S((negs, fg), BF16),
+            S((CH, pn.slab), BF16),
+            S(meta.shape, F32),
+            S((2 * nj, rows, 256), F32),
+            S((2 * nj, rows, 256), BF16),
+            S((rows, emb), F32),
+            S((rows, emb), BF16),
+            S((rows, emb), BF16),
+            S((emb, rows), BF16),
+            S((rows, width), F32),
+            S((rows, emb), F32),
+            S((n_dp, rows, width), F32),
+            S((n_all, emb, width // 2), F32),
+            S((rounds + 1, 2, n_dp, width), F32),
+            S((rounds, 2, n_dp, width), F32),
+            S((n_dp, width), F32),
+            S((n_dp, width), F32),
+            S((feats, rows), BF16),
+            S((2 * nj, rows, 256), BF16),
+            S((rows, emb), BF16),
+            S((sends, 256), BF16),
+            S((n_dp * nj * CH, 256), BF16),
+            S((n_all - 1, emb, width // 2), BF16),
+            S((n_all - 1, emb, width // 2), BF16),
+            S((n_dp, hp, emb), F32),
+            S((n_all - 1, hp, emb), BF16),
+            S((n_all - 1, hp, emb), BF16),
+            S((n_dp, hp, emb), BF16),
+            pltpu.SemaphoreType.DMA((16,)),
+            pltpu.SemaphoreType.DMA((n_sem,)),
+            pltpu.SemaphoreType.DMA((n_sem,)),
+        ],
+        compiler_params=pltpu.CompilerParams(
+            collective_id=2, has_side_effects=True, vmem_limit_bytes=62 << 20),
+        name="fused",
+    )(queries, items, corpus, meta, w1, w2)
+    return loss.reshape(-1), gq, gw1, gw2
+
+
+def fits(n_dp, groups, queries, items, corpus, sample_ids, w1, w2):
+    negs = sample_ids.shape[0] // groups
+    return (
+        groups == 2 and n_dp == 16 and queries.shape == (256, 256)
+        and negs % CH == 0 and negs >= 2 * CH
+        and w1.shape == (n_dp * CH, 512) and w2.shape == (512, 256)
+        and items.shape[1] * 2 == w1.shape[0] and corpus.shape[0] % 256 == 0
+    )
+
+
 def per_device(queries, item_features, corpus, sample_ids, sample_shift, w1, w2):
     groups = lax.axis_size("group")
     member = lax.axis_index("group")
     n_dp = lax.axis_size("dp")
     d = lax.axis_index("dp")
+    if fits(n_dp, groups, queries, item_features, corpus, sample_ids, w1, w2):
+        return fused(n_dp, queries, item_features, corpus, sample_ids, sample_shift, w1, w2)
     query_rows, emb = queries.shape
     quota = query_rows // groups
     negs = sample_ids.shape[0] // groups

time: 228 us -> 159 us (0.70)
  Pallas kernels: 106 us -> 148 us
  waiting for transfers between devices: 29.7 us -> 0 us
  local copies, waits for them, and re-layouts: 33.4 us -> 8.15 us
  matrix products: 20.8 us -> 0 us
  between operations: 14.3 us -> 0.64 us
  other arithmetic: 15.4 us -> 1.97 us
  starting transfers between devices: 7.46 us -> 0 us
    pallas_call x2 -> x1, Pallas kernels: 106 us -> 148 us  [fused(): pl.pallas_call(functools.partial(fused_kernel, pn, rows), out_shape=(jax....]
    ppermute x7 -> x0, waiting for transfers between devices: 29.7 us -> none  [the longest x4 29.7 us: shift(): lax.ppermute(x, 'group', [(i, (i + s) % groups) for i in range(groups)])]
    dot_general x6 -> x0, matrix products: 20.8 us -> none  [the longest x4 11.7 us: mm(): return jnp.dot(a, b, preferred_element_type=F32)]
    gather x2 -> x0, local copies, waits for them, and re-layouts: 11.7 us -> none  [the longest x1 6.21 us: per_device(): own_rows = corpus.at[at(ids, member)].get(mode='promise_in_bounds')]
    convert_element_type x6 -> x0, other arithmetic: 8.8 us -> none  [the longest x2 3.93 us: per_device(): normed = (embedded * inverse).astype(BF16)]
    ppermute x7 -> x0, starting transfers between devices: 7.42 us -> none  [the longest x4 5.79 us: shift(): lax.ppermute(x, 'group', [(i, (i + s) % groups) for i in range(groups)])]
    slice x4 -> x0, local copies, waits for them, and re-layouts: 3.33 us -> none  [per_device(): w1s.append(jnp.concatenate([p[:w1_rows] for p in placed], 0))]
    select_n x4 -> x0, other arithmetic: 3.15 us -> none  [the longest x2 1.69 us: place_columns(): jnp.where(swap, parts[0], parts[1])]
  transfers between devices with their start and end apart: 8 -> 0, of which waited for: 3 -> 0; matrix products, arithmetic and copies ran while one was open for 20% -> 0% of each run, Pallas kernels for 0% -> 0%
where the time goes in v1:
time: 159 us
  Pallas kernels  148 us (93%)
  local copies, waits for them, and re-layouts  8.15 us (5%)
  other arithmetic  1.97 us (1%)
    pallas_call x1, Pallas kernels, fused(): pl.pallas_call(functools.partial(fused_kernel, pn, rows), out_shape=(jax....  148 us
    unnamed x6, local copies, waits for them, and re-layouts  8.15 us

profile of v1, /device:TPU:0, one launch (start us, length us, event | category | flops | bytes accessed | tf_op | source)
XLA Modules:
  0.0 158.7 jit_solution(13306696869007846919)
XLA Ops:
  0.6 0.7 convert_bitcast_fusion
  1.3 0.7 bitcast_convert_fusion
  2.0 0.6 pad_maximum_fusion.meta_in
  2.6 147.9 %fused.1 = (f32[1,128]{1,0:T(1,128)}, f32[128,256]{1,0:T(8,128)}, f32[2048,512]{1,0:T(8,128)}, f32[512,256]{1,0:T(8,128)}) custom-call(bf16[256,256]{1,0:T(8,128)(2,1)} %queries.1, bf16[256,1024]{1,0:T(8,128)(2,1)} %items.1, bf16[2048,1024]{1,0:T(8,128)(2,1)} %corpus.1, f32[16,128]{1,0:T(8,128)} %pad_maximum_fusion.meta_in, bf16[2048,512]{1,0:T(8,128)(2,1)} %w1.1, ...), custom_call_target="tpu_custom_call" | custom-call | tf_op jit(solution)/shard_map/fused/pallas_call | solution.py:785
  150.5 1.1 copy.15
  151.6 1.6 copy.16
  153.2 0.0 copy-start
  153.2 4.7 %copy.17 = f32[2048,512]{1,0:T(8,128)} copy(f32[2048,512]{1,0:T(8,128)} %get-tuple-element.18) | data formatting | bytes 8388608
  157.9 0.0 copy-done
  157.9 0.8 copy.18
Async XLA Ops:
  153.2 4.7 %copy-start = (f32[512,256]{1,0:T(8,128)S(1)}, f32[512,256]{1,0:T(8,128)}, u32[]{:S(2)}) copy-start(f32[512,256]{1,0:T(8,128)} %get-tuple-element.19) | copy-start | bytes 1572868

commit v2 on v1

--- a/solution.py
+++ b/solution.py
@@ -291,7 +291,8 @@
         core, x, z = bits[0], bits[1], bits[2:]
         dp = lambda steps: [("dp", s) for s in steps]
         y = [("group", 1)]
-        self.gather_order = [x] + z[::-1] + [core]
+        self.gather_orders = [[x] + z[::-1] + [core], z[::-1] + [x, core]]
+        self.w_gather = [z[0], x, core]
         self.q_order = dp([core, x]) + y + dp(z)
         self.w_orders = [
             dp([core]) + y + dp([x]) + dp(z),
@@ -303,12 +304,13 @@
 
 
 PART_ROWS = (0, 48, 96, 128)
+ROW_PARTS = (0, 384, 512, 640)
 CH = 128
 
 
-def fused_kernel(pn, rows, queries, items, corpus, meta_in, w1, w2,
+def fused_kernel(pn, rows, queries, items, corpus, ids_in, shift_in, w1, w2,
                  loss_ref, gq_ref, gw1_ref, gw2_ref,
-                 big, q_all, w1v, w2v, mine, peer, far, hot, meta, pre, hid, emb, nrm, nrms, nrm_t,
+                 big, q_all, w1v, w2v, mine, peer, far, hot, ids_v, shift_v, pre, hid, emb, nrm, nrms, nrm_t,
                  bias, hat, logits, qpt, stats, arrived, total_ref, fac, featt, gp, ge,
                  recv, ag, qsend, qrecv, acc2, send2, recv2, ag2, lsem, ssem, rsem):
     n_dp, width, fg, hg, slab = pn.n_dp, pn.query_rows, pn.fg, pn.hg, pn.slab
@@ -339,12 +341,12 @@
         copy.start()
         return copy
 
-    gw = {s: 1 << k for k, s in enumerate(pn.gather_order)}
-    pos = sum(bit(s) * gw[s] for s in pn.bits)
+    gws = [{s: 1 << k for k, s in enumerate(order)} for order in pn.gather_orders]
+    poss = [sum(bit(s) * gw[s] for s in pn.bits) for gw in gws]
     tiles = n_dp
 
-    c_q = local(queries, q_all.at[pos])
-    c_meta = local(meta_in, meta)
+    c_q = [local(queries.at[g * quota : (g + 1) * quota], q_all.at[g, poss[g]]) for g in range(2)]
+    c_meta = [local(ids_in, ids_v), local(shift_in, shift_v)]
     c_slab = [local(corpus.at[:, n * 256 : (n + 1) * 256], big.at[n * slab : (n + 1) * slab])
               for n in range(fg // 256)]
     c_mine = local(items.at[pl.ds(pl.multiple_of(m * quota, quota), quota)], mine.at[0:quota])
@@ -352,31 +354,57 @@
     c_w2 = local(w2, w2v.at[0])
     greet([partner(a, b)[1] for a, b in rounds])
 
-    e = bit(core) * 2 + bit(xbit)
-    q1, q2 = w1.shape[0] // 4, w2.shape[0] // 4
-
-    def span(n, base, size):
-        return pl.ds(pl.multiple_of(base * n, n), n * size)
-
-    wy = [remote(w1.at[span(q1, e, 1)], w1v.at[1, span(q1, e, 1)], ypeer),
-          remote(w2.at[span(q2, e, 1)], w2v.at[1, span(q2, e, 1)], ypeer)]
-    for c in wy:
-        c.start()
+    class Spread:
+        def __init__(self, first, follow, n):
+            self.follow, self.n, self.k = follow, n, 0
+            self.live = first
+            for c in first:
+                c.start()
+
+        def go(self):
+            for c in self.live:
+                c.wait()
+            self.live = []
+            if self.k < self.n:
+                self.live = self.follow(self.k)
+                for c in self.live:
+                    c.start()
+                self.k += 1
+
+    n_piece = 1 << len(pn.w_gather)
+    e = sum(bit(s) << k for k, s in enumerate(pn.w_gather))
+    q1, q2 = fg // n_piece, hg // 2 // n_piece
+
+    def w_rows(half, size):
+        base = lax.div(e, size) * size
+        return (pl.ds(pl.multiple_of(half * fg + base * q1, q1), size * q1),
+                pl.ds(pl.multiple_of(half * (hg // 2) + base * q2, q2), size * q2))
+
+    def w_spread(half, far_half):
+        a, b = w_rows(far_half, 1)
+
+        def follow(k):
+            at1, at2 = w_rows(half, 1 << k)
+            to = partner("dp", pn.w_gather[k])[1]
+            return [remote(w1v.at[1, at1], w1v.at[1, at1], to),
+                    remote(w2v.at[1, at2], w2v.at[1, at2], to)]
+
+        return Spread([remote(w1.at[a], w1v.at[1, a], ypeer), remote(w2.at[b], w2v.at[1, b], ypeer)],
+                      follow, len(pn.w_gather))
+
+    def q_spread(g):
+        def follow(k):
+            view = q_all.at[g, pl.ds(lax.div(poss[g], 1 << k) * (1 << k), 1 << k)]
+            return [remote(view, view, partner("dp", pn.gather_orders[g][k])[1])]
+
+        return Spread(follow(0), lambda k: follow(k + 1), len(pn.bits) - 1)
+
+    ws = [w_spread(m, other), w_spread(other, m)]
+    for c in c_q:
+        c.wait()
+    qs = [q_spread(0), q_spread(1)]
     item_send = remote(items.at[pl.ds(pl.multiple_of(other * quota, quota), quota)],
                        peer.at[0:quota], ypeer)
-    item_send.start()
-    c_q.wait()
-    q_steps = pn.gather_order
-
-    def q_gather(k):
-        size = 1 << k
-        base = lax.div(pos, size) * size
-        view = q_all.at[pl.ds(base, size)]
-        c = remote(view, view, partner("dp", q_steps[k])[1])
-        c.start()
-        return c
-
-    qg = q_gather(0)
     k_far = [next(count) for _ in range(chunks)][0]
 
     def rows_at(k):
@@ -386,39 +414,41 @@
         return remote(far.at[pl.ds(pl.multiple_of(k * CH, CH), CH)], peer.at[rows_at(k)],
                       ypeer, k_far + k)
 
-    def column(r):
-        return jnp.broadcast_to(meta[pl.ds(r, 1), :], (8, CH)).T[:, :1]
+    def column(ref, r):
+        return jnp.broadcast_to(ref[pl.ds(r, 1), :].astype(F32), (8, CH)).T[:, :1]
 
     def pick(who, k, dst, at):
-        ids = column(who * chunks + k)
+        ids = column(ids_v, who * chunks + k)
         where = lax.broadcasted_iota(jnp.int32, (CH, slab), 1).astype(F32)
         hot[...] = jnp.where(ids == where, 1.0, 0.0).astype(BF16)
         for n in range(fg // 256):
             dst[at, n * 256 : (n + 1) * 256] = mm(
                 hot[...], big[n * slab : (n + 1) * slab, :]).astype(BF16)
 
-    c_meta.wait()
-    for c in c_slab:
+    for c in c_meta + c_slab:
         c.wait()
-
-    def pick_far(k):
-        pick(other, k, far, pl.ds(pl.multiple_of(k * CH, CH), CH))
-        far_copy(k).start()
-
-    loop(chunks, pick_far)
-    qg.wait()
-    qg = q_gather(1)
+    loop(chunks, lambda k: pick(other, k, far, pl.ds(pl.multiple_of(k * CH, CH), CH)))
+    qs[0].go()
+    qs[1].go()
+    ws[0].go()
+    ws[1].go()
+    item_send.start()
+    loop(chunks, lambda k: far_copy(k).start())
     loop(chunks, lambda k: pick(m, k, mine, rows_at(k)))
+    qs[1].go()
+    ws[0].go()
+    qs[0].go()
     bias[0:quota, :] = jnp.zeros((quota, width), F32)
 
     def put_bias(k):
         bias[rows_at(k), :] = jnp.broadcast_to(
-            -column(2 * chunks + m * chunks + k), (CH, width))
+            -column(shift_v, m * chunks + k), (CH, width))
 
     loop(chunks, put_bias)
     c_mine.wait()
     c_w1.wait()
     c_w2.wait()
+    ws[1].go()
 
     nj = hg // 256
 
@@ -432,33 +462,19 @@
                 pre[c * nj + j, r0:r1, :] += part
 
     tower_add(0, rows, mine, m, 0, True)
-    for c in wy:
-        c.wait()
-    pair = lax.div(e, 2) * 2
-    wx = [remote(w1v.at[1, span(q1, e, 1)], w1v.at[1, span(q1, e, 1)], partner("dp", xbit)[1]),
-          remote(w2v.at[1, span(q2, e, 1)], w2v.at[1, span(q2, e, 1)], partner("dp", xbit)[1])]
-    for c in wx:
-        c.start()
-    for k in range(2, len(q_steps) - 1):
-        qg.wait()
-        qg = q_gather(k)
+    qs[1].go()
+    qs[0].go()
 
     def turn(src, half, n):
         at = pl.multiple_of(n * 256, 256)
         featt[pl.ds(pl.multiple_of(half * fg + at, 256), 256), :] = src[:, pl.ds(at, 256)].T
 
+    ws[0].go()
     loop(fg // 256, lambda n: turn(mine, m, n))
-    for c in wx:
-        c.wait()
-    wc = [remote(w1v.at[1, span(q1, pair, 2)], w1v.at[1, span(q1, pair, 2)], partner("dp", core)[1]),
-          remote(w2v.at[1, span(q2, pair, 2)], w2v.at[1, span(q2, pair, 2)], partner("dp", core)[1])]
-    for c in wc:
-        c.start()
-    qg.wait()
-    qg = q_gather(len(q_steps) - 1)
-    for c in wc:
-        c.wait()
+    ws[1].go()
+    ws[0].go()
     tower_add(0, rows, mine, m, 1, True)
+    ws[1].go()
 
     def finish_tower(r0, r1):
         loop(2, lambda c: tower_add(r0, r1, peer, other, c, False))
@@ -481,53 +497,57 @@
     oq = weights_of(pn.q_order)
     gq = oq[("group", 1)]
 
-    def shard_of(i):
-        return sum(lax.rem(lax.div(i, gw[s]), 2) * oq[("dp", s)] for s in pn.bits)
-
-    ra = rows - CH
+    def shard_of(i, g):
+        return g * gq + sum(
+            lax.rem(lax.div(i, gws[g][s]), 2) * oq[("dp", s)] for s in pn.bits)
+
     half_q = width // 2
 
-    def score_a(i):
-        block = nt(nrms[0:ra, :], q_all[i]) + bias[0:ra, :]
-        logits[i, 0:ra, :] = block
-        top = jnp.max(block, 0, keepdims=True)
-        p = jnp.exp(block - top)
-        stats[0, 0, pl.ds(i, 1), :] = top
-        stats[0, 1, pl.ds(i, 1), :] = jnp.sum(p, 0, keepdims=True)
-        part = mm(nrm_t[:, 0:ra], p.astype(BF16))
-        j = shard_of(i)
+    def queries_at(i):
+        return jnp.concatenate([q_all[0, i], q_all[1, i]], 0)
+
+    def score(r0, r1):
+        def one(i):
+            block = nt(nrms[r0:r1, :], queries_at(i)) + bias[r0:r1, :]
+            logits[i, r0:r1, :] = block
+            top = jnp.max(block, 0, keepdims=True)
+            at = pl.ds(i, 1)
+            if r0 == 0:
+                stats[0, 1, at, :] = jnp.sum(jnp.exp(block - top), 0, keepdims=True)
+            else:
+                before = stats[0, 0, at, :]
+                top = jnp.maximum(before, top)
+                stats[0, 1, at, :] = stats[0, 1, at, :] * jnp.exp(before - top) + jnp.sum(
+                    jnp.exp(block - top), 0, keepdims=True)
+            stats[0, 0, at, :] = top
+
+        loop(tiles, one)
+
+    item_send.wait()
+    done = 0
+    for r0, r1 in zip(ROW_PARTS[:-1], ROW_PARTS[1:]):
+        upto = (r1 - quota) // CH
+        for k in range(done, upto):
+            far_copy(k).wait()
+        done = upto
+        finish_tower(r0, r1)
+        if r0 == 0:
+            qs[0].go()
+            qs[1].go()
+        score(r0, r1)
+
+    def query_part(i):
+        p = jnp.exp(logits[i] - stats[0, 0, pl.ds(i, 1), :])
+        part = mm(nrm_t[...], p.astype(BF16))
         for g in range(2):
-            qpt[j + g * gq] = part[:, g * half_q : (g + 1) * half_q]
-
-    def score_b(i):
-        block = nt(nrms[ra:rows, :], q_all[i]) + bias[ra:rows, :]
-        logits[i, ra:rows, :] = block
-        before = stats[0, 0, pl.ds(i, 1), :]
-        top = jnp.maximum(before, jnp.max(block, 0, keepdims=True))
-        shrink = jnp.exp(before - top)
-        p = jnp.exp(block - top)
-        stats[0, 0, pl.ds(i, 1), :] = top
-        stats[0, 1, pl.ds(i, 1), :] = (
-            stats[0, 1, pl.ds(i, 1), :] * shrink + jnp.sum(p, 0, keepdims=True))
-        part = mm(nrm_t[:, ra:rows], p.astype(BF16))
-        j = shard_of(i)
-        for g in range(2):
-            cut = slice(g * half_q, (g + 1) * half_q)
-            qpt[j + g * gq] = qpt[j + g * gq] * shrink[:, cut] + part[:, cut]
-
-    item_send.wait()
-    loop(chunks - 1, lambda k: far_copy(k).wait())
-    finish_tower(0, ra)
-    qg.wait()
-    loop(tiles, score_a)
-    far_copy(chunks - 1).wait()
-    finish_tower(ra, rows)
-    loop(tiles, score_b)
+            qpt[shard_of(i, g)] = part[:, g * half_q : (g + 1) * half_q]
 
     for r, (axis, step) in enumerate(rounds):
         copy = remote(stats.at[r], arrived.at[r], partner(axis, step)[1])
         copy.start()
-        if r == 0:
+        if r < 4:
+            loop(tiles // 4, lambda i: query_part(r * (tiles // 4) + i))
+        else:
             loop(fg // 256, lambda n: turn(peer, other, n))
         copy.wait()
         m0, s0, m1, s1 = stats[r, 0], stats[r, 1], arrived[r, 0], arrived[r, 1]
@@ -585,9 +605,9 @@
 
     def scale_q(i):
         f = fac[pl.ds(i, 1), :]
-        j = shard_of(i)
         for g in range(2):
-            qpt[j + g * gq] = qpt[j + g * gq] * f[:, g * half_q : (g + 1) * half_q]
+            j = shard_of(i, g)
+            qpt[j] = qpt[j] * f[:, g * half_q : (g + 1) * half_q]
 
     loop(tiles, scale_q)
     loop(n_dp, lambda j: q_put(j, (1 - 2 * cb) * n_dp + j))
@@ -597,12 +617,14 @@
 
     def second(i):
         p = jnp.exp(logits[i] - total_ref[pl.ds(i, 1), :]).astype(BF16)
-        hat[...] += mm(p, q_all[i])
-
-    loop(tiles, second)
+        hat[...] += mm(p, queries_at(i))
+
+    loop(tiles // 2, second)
     q_chain.step(1)
-
-    q_own = q_all[pos, pl.ds(pl.multiple_of(m * quota, quota), quota), :].astype(F32)
+    loop(tiles // 2, lambda i: second(tiles // 2 + i))
+
+    pos = jnp.where(m == 0, poss[0], poss[1])
+    q_own = q_all[m, pos].astype(F32)
     positive = nrm[0:quota, :].astype(F32)
     mine_total = total_ref[pl.ds(pos, 1), :]
     mine_total = jnp.where(m == 0, mine_total[:, :half_q], mine_total[:, half_q:])
@@ -703,9 +725,9 @@
         ch.begin(0)
     w2_half(1 - cb, w2_send)
     w2_chain.begin(0)
-    q_chain.step(2)
     w1_half(cb, sink_acc)
     w2_half(cb, w2_acc)
+    q_chain.step(2)
     every = chains + [w2_chain]
     steps = len(pn.w2_order)
     for r in range(1, steps + 1):
@@ -760,10 +782,10 @@
             for t in range(nj):
                 at = n_dp * nj * p0 + fb * (nj * pr) + t * pr
                 gw1_ref[pl.ds(pl.multiple_of(fb * CH + p0, 16), pr), t * 256 : (t + 1) * 256] = ag[
-                    pl.ds(pl.multiple_of(at, 16), pr), :].astype(F32)
+                    pl.ds(pl.multiple_of(at, 16), pr), :]
 
         loop(n_dp, out_rows)
-    gw2_ref[...] = ag2[...].reshape(gw2_ref.shape).astype(F32)
+    gw2_ref[...] = ag2[...].reshape(gw2_ref.shape)
 
 
 def fused(n_dp, queries, items, corpus, sample_ids, sample_shift, w1, w2):
@@ -775,7 +797,8 @@
     nj = hg // 256
     n_all = 2 * n_dp
     rounds = n_all.bit_length() - 1
-    meta = jnp.concatenate([sample_ids.astype(F32), sample_shift.astype(F32)]).reshape(-1, CH)
+    ids = sample_ids.reshape(-1, CH)
+    shifts = sample_shift.astype(F32).reshape(-1, CH)
     half = feats // 2
     sends = (n_all - 1) * nj * CH
     big = -(-max(sends, (fg // 256) * pn.slab) // 16) * 16
@@ -787,21 +810,22 @@
         out_shape=(
             jax.ShapeDtypeStruct((1, pn.quota), F32),
             jax.ShapeDtypeStruct((pn.quota, emb), F32),
-            jax.ShapeDtypeStruct((feats, hg), F32),
-            jax.ShapeDtypeStruct((hg, emb), F32),
+            jax.ShapeDtypeStruct((feats, hg), BF16),
+            jax.ShapeDtypeStruct((hg, emb), BF16),
         ),
-        in_specs=[ANY] * 6,
+        in_specs=[ANY] * 7,
         out_specs=(VMEM,) * 4,
         scratch_shapes=[
             S((big, 256), BF16),
-            S((n_dp, width, emb), BF16),
+            S((2, n_dp, width // 2, emb), BF16),
             S((2, feats, hg), BF16),
             S((2, hg, emb), BF16),
             S((rows, fg), BF16),
             S((rows, fg), BF16),
             S((negs, fg), BF16),
             S((CH, pn.slab), BF16),
-            S(meta.shape, F32),
+            S(ids.shape, jnp.int32),
+            S(shifts.shape, F32),
             S((2 * nj, rows, 256), F32),
             S((2 * nj, rows, 256), BF16),
             S((rows, emb), F32),
@@ -834,15 +858,36 @@
         compiler_params=pltpu.CompilerParams(
             collective_id=2, has_side_effects=True, vmem_limit_bytes=62 << 20),
         name="fused",
-    )(queries, items, corpus, meta, w1, w2)
-    return loss.reshape(-1), gq, gw1, gw2
+    )(queries, items, corpus, ids, shifts, w1, w2)
+    return widen(loss, gq, gw1, gw2)
+
+
+def widen_kernel(*refs):
+    n = len(refs) // 2
+    for a, b in zip(refs[:n], refs[n:]):
+        b[...] = a[...].astype(F32)
+
+
+def widen(loss, *grads):
+    parts = 4
+    specs = [pl.BlockSpec(loss.shape, lambda i: (0, 0))] + [
+        pl.BlockSpec((x.shape[0] // parts, x.shape[1]), lambda i: (i, 0)) for x in grads]
+    loss, *grads = pl.pallas_call(
+        widen_kernel,
+        grid=(parts,),
+        out_shape=tuple(jax.ShapeDtypeStruct(x.shape, F32) for x in (loss, *grads)),
+        in_specs=specs,
+        out_specs=tuple(specs),
+        name="widen",
+    )(loss, *grads)
+    return (loss.reshape(-1), *grads)
 
 
 def fits(n_dp, groups, queries, items, corpus, sample_ids, w1, w2):
     negs = sample_ids.shape[0] // groups
     return (
         groups == 2 and n_dp == 16 and queries.shape == (256, 256)
-        and negs % CH == 0 and negs >= 2 * CH
+        and (256 // groups + negs) == ROW_PARTS[-1]
         and w1.shape == (n_dp * CH, 512) and w2.shape == (512, 256)
         and items.shape[1] * 2 == w1.shape[0] and corpus.shape[0] % 256 == 0
     )

time: 159 us -> 151 us (0.950)
  local copies, waits for them, and re-layouts: 8.15 us -> 0 us
    unnamed x6 -> x0, local copies, waits for them, and re-layouts: 8.15 us -> none
    pallas_call x0 -> x1, Pallas kernels: none -> 4.34 us  [widen(): pl.pallas_call(widen_kernel, grid=(parts,), out_shape=tuple((jax.ShapeDty...]
    pallas_call x1, Pallas kernels: 148 us -> 145 us  [fused(): pl.pallas_call(functools.partial(fused_kernel, pn, rows), out_shape=(jax....]
    concatenate x3 -> x0, other arithmetic: 1.97 us -> none  [fused(): jnp.concatenate([sample_ids.astype(F32), sample_shift.astype(F32)])]
where the time goes in v2:
time: 151 us
  Pallas kernels  149 us (99%)
    pallas_call x1, Pallas kernels, fused(): pl.pallas_call(functools.partial(fused_kernel, pn, rows), out_shape=(jax....  145 us
    pallas_call x1, Pallas kernels, widen(): pl.pallas_call(widen_kernel, grid=(parts,), out_shape=tuple((jax.ShapeDty...  4.34 us

profile of v2, /device:TPU:0, one launch (start us, length us, event | category | flops | bytes accessed | tf_op | source)
XLA Modules:
  0.0 151.2 jit_solution(15185251732681436312)
XLA Ops:
  0.6 1.3 bitcast_convert_fusion.shift_in
  1.9 145.0 %fused.1 = (f32[1,128]{1,0:T(1,128)}, f32[128,256]{1,0:T(8,128)}, bf16[2048,512]{1,0:T(8,128)(2,1)}, bf16[512,256]{1,0:T(8,128)(2,1)}) custom-call(bf16[256,256]{1,0:T(8,128)(2,1)} %queries.1, bf16[256,1024]{1,0:T(8,128)(2,1)} %items.1, bf16[2048,1024]{1,0:T(8,128)(2,1)} %corpus.1, s32[8,128]{1,0:T(8,128)} %bitcast.5, ...), custom_call_target="tpu_custom_call" | custom-call | tf_op jit(solution)/shard_map/fused/pallas_call | solution.py:808
  146.9 4.3 %widen.1 = (f32[1,128]{1,0:T(1,128)}, f32[128,256]{1,0:T(8,128)}, f32[2048,512]{1,0:T(8,128)}, f32[512,256]{1,0:T(8,128)}) custom-call(f32[1,128]{1,0:T(1,128)} %get-tuple-element.12.refs_0_, f32[128,256]{1,0:T(8,128)} %get-tuple-element.13.refs_1_, bf16[2048,512]{1,0:T(8,128)(2,1)} %get-tuple-element.14.refs_2_, bf16[512,256]{1,0:T(8,128)(2,1)} %get-tuple-element.15.refs_3_), custom_call_target="tpu_custom_call" | custom-call | tf_op jit(solution)/shard_map/widen/pallas_call | solution.py:875

commit v3 on v2

--- a/solution.py
+++ b/solution.py
@@ -275,6 +275,15 @@
     lax.fori_loop(0, n, step, 0)
 
 
+def loop_by(k, n, body):
+    def step(i, carry):
+        for u in range(k):
+            body(i * k + u)
+        return carry
+
+    lax.fori_loop(0, n // k, step, 0)
+
+
 def weights_of(order):
     return {axis_step: 1 << (len(order) - 1 - k) for k, axis_step in enumerate(order)}
 
@@ -293,17 +302,18 @@
         y = [("group", 1)]
         self.gather_orders = [[x] + z[::-1] + [core], z[::-1] + [x, core]]
         self.w_gather = [z[0], x, core]
-        self.q_order = dp([core, x]) + y + dp(z)
-        self.w_orders = [
-            dp([core]) + y + dp([x]) + dp(z),
-            dp([core, x]) + y + dp(z),
-            dp([core]) + dp(z) + dp([x]) + y,
+        self.q_orders = [dp([core, x]) + y + dp(z), dp([core]) + y + dp([x]) + dp(z)]
+        zn, zf = z[:1], z[1:]
+        self.parts = [
+            (48, dp([core]) + y + dp(zn + [x] + zf), z[::-1] + [x, core]),
+            (16, dp([core, x]) + y + dp(z), z[::-1] + [x, core]),
+            (32, dp([core, x]) + y + dp(z), [x] + z[::-1] + [core]),
+            (32, dp([core] + zn + [x] + zf) + y, zf[::-1] + [x] + zn + [core]),
         ]
-        self.w2_order = self.w_orders[1]
+        self.w2_part = (dp([core] + zn + [x]) + y + dp(zf), z[::-1] + [x, core])
         self.bits = bits
 
 
-PART_ROWS = (0, 48, 96, 128)
 ROW_PARTS = (0, 384, 512, 640)
 CH = 128
 
@@ -405,6 +415,7 @@
     qs = [q_spread(0), q_spread(1)]
     item_send = remote(items.at[pl.ds(pl.multiple_of(other * quota, quota), quota)],
                        peer.at[0:quota], ypeer)
+    item_send.start()
     k_far = [next(count) for _ in range(chunks)][0]
 
     def rows_at(k):
@@ -432,7 +443,6 @@
     qs[1].go()
     ws[0].go()
     ws[1].go()
-    item_send.start()
     loop(chunks, lambda k: far_copy(k).start())
     loop(chunks, lambda k: pick(m, k, mine, rows_at(k)))
     qs[1].go()
@@ -494,12 +504,12 @@
         nrms[r0:r1, :] = (no.astype(F32) * scale).astype(BF16)
         nrm_t[:, r0:r1] = no.astype(F32).T.astype(BF16)
 
-    oq = weights_of(pn.q_order)
-    gq = oq[("group", 1)]
-
-    def shard_of(i, g):
-        return g * gq + sum(
-            lax.rem(lax.div(i, gws[g][s]), 2) * oq[("dp", s)] for s in pn.bits)
+    oqs = [weights_of(order) for order in pn.q_orders]
+    he = e_dim // 2
+
+    def shard_of(i, g, h):
+        return g * oqs[h][("group", 1)] + sum(
+            lax.rem(lax.div(i, gws[g][s]), 2) * oqs[h][("dp", s)] for s in pn.bits)
 
     half_q = width // 2
 
@@ -521,7 +531,7 @@
                     jnp.exp(block - top), 0, keepdims=True)
             stats[0, 0, at, :] = top
 
-        loop(tiles, one)
+        loop_by(4, tiles, one)
 
     item_send.wait()
     done = 0
@@ -540,13 +550,15 @@
         p = jnp.exp(logits[i] - stats[0, 0, pl.ds(i, 1), :])
         part = mm(nrm_t[...], p.astype(BF16))
         for g in range(2):
-            qpt[shard_of(i, g)] = part[:, g * half_q : (g + 1) * half_q]
+            for h in range(2):
+                qpt[h, shard_of(i, g, h)] = part[
+                    h * he : (h + 1) * he, g * half_q : (g + 1) * half_q]
 
     for r, (axis, step) in enumerate(rounds):
         copy = remote(stats.at[r], arrived.at[r], partner(axis, step)[1])
         copy.start()
         if r < 4:
-            loop(tiles // 4, lambda i: query_part(r * (tiles // 4) + i))
+            loop_by(2, tiles // 4, lambda i: query_part(r * (tiles // 4) + i))
         else:
             loop(fg // 256, lambda n: turn(peer, other, n))
         copy.wait()
@@ -565,53 +577,73 @@
             self.n = 1 << len(order)
             self.base = 0
 
-        def begin(self, r):
+        def launch(self, r):
             half = self.n >> (r + 1)
             at0 = self.n - 2 * half
-            b, to = partner(*self.order[r])
-            if r > 0:
-                base = self.base
-                loop(half, lambda j: self.put(at0 + j, base + (1 - b) * half + j))
-            self.copy = remote(self.send_at(at0, half), self.recv_at(at0, half), to)
+            self.copy = remote(self.send_at(at0, half), self.recv_at(at0, half),
+                               partner(*self.order[r])[1])
             self.copy.start()
 
-        def finish(self, r):
+        def send(self, r):
             half = self.n >> (r + 1)
-            at0 = self.n - 2 * half
-            b, _ = partner(*self.order[r])
+            at0, came = self.n - 2 * half, self.n - 4 * half
             self.copy.wait()
-            if r > 0:
-                self.base = self.base + b * half
-            base = self.base
-            loop(half, lambda j: self.add(base + j, at0 + j))
-
-        def step(self, r):
-            if r > 0:
-                self.finish(r - 1)
-            if r < len(self.order):
-                self.begin(r)
+            skip = (1 - partner(*self.order[r])[0]) * half
+            base = self.base + skip
+            loop_by(min(4, half), half, lambda j: self.put(at0 + j, base + j, came + skip + j))
+            self.launch(r)
+
+        def keep(self, r):
+            half = self.n >> (r + 1)
+            came = self.n - 4 * half
+            skip = partner(*self.order[r])[0] * half
+            base = self.base + skip
+            loop_by(min(4, half), half, lambda j: self.add(base + j, came + skip + j))
+            self.base = base
+
+        def finish(self):
+            self.copy.wait()
+            self.add(self.base, self.n - 2)
+
+    def advance(some, r):
+        for ch in some:
+            if r < len(ch.order):
+                ch.send(r)
+            else:
+                ch.finish()
+        for ch in some:
+            if r < len(ch.order):
+                ch.keep(r)
 
     cb = bit(core)
     own16 = cb * n_dp
 
-    def q_put(slot, a):
-        qsend[slot] = qpt[own16 + a].astype(BF16)
-
-    def q_add(a, slot):
-        qpt[own16 + a] = qpt[own16 + a] + qrecv[slot].astype(F32)
-
-    q_chain = Chain(pn.q_order, q_put, q_add,
-                    lambda a, n: qsend.at[pl.ds(a, n)], lambda a, n: qrecv.at[pl.ds(a, n)])
+    def q_chain(h):
+        def put(slot, a, got):
+            qsend[h, slot] = (qpt[h, own16 + a] + qrecv[h, got].astype(F32)).astype(BF16)
+
+        def add(a, got):
+            qpt[h, own16 + a] = qpt[h, own16 + a] + qrecv[h, got].astype(F32)
+
+        return Chain(pn.q_orders[h], put, add,
+                     lambda a, n: qsend.at[h, pl.ds(a, n)], lambda a, n: qrecv.at[h, pl.ds(a, n)])
+
+    q_chains = [q_chain(0), q_chain(1)]
 
     def scale_q(i):
         f = fac[pl.ds(i, 1), :]
         for g in range(2):
-            j = shard_of(i, g)
-            qpt[j] = qpt[j] * f[:, g * half_q : (g + 1) * half_q]
-
-    loop(tiles, scale_q)
-    loop(n_dp, lambda j: q_put(j, (1 - 2 * cb) * n_dp + j))
-    q_chain.begin(0)
+            for h in range(2):
+                j = shard_of(i, g, h)
+                qpt[h, j] = qpt[h, j] * f[:, g * half_q : (g + 1) * half_q]
+
+    def q_first(h, j):
+        qsend[h, j] = qpt[h, (1 - cb) * n_dp + j].astype(BF16)
+
+    loop_by(4, tiles, scale_q)
+    for h in range(2):
+        loop_by(4, n_dp, functools.partial(q_first, h))
+        q_chains[h].launch(0)
 
     hat[...] = jnp.zeros_like(hat)
 
@@ -619,9 +651,9 @@
         p = jnp.exp(logits[i] - total_ref[pl.ds(i, 1), :]).astype(BF16)
         hat[...] += mm(p, queries_at(i))
 
-    loop(tiles // 2, second)
-    q_chain.step(1)
-    loop(tiles // 2, lambda i: second(tiles // 2 + i))
+    loop_by(4, tiles // 2, second)
+    advance(q_chains, 1)
+    loop_by(4, tiles // 2, lambda i: second(tiles // 2 + i))
 
     pos = jnp.where(m == 0, poss[0], poss[1])
     q_own = q_all[m, pos].astype(F32)
@@ -648,54 +680,54 @@
     per_core = n_dp // 2
     n_all = 2 * n_dp
 
-    def place(fb, g, order):
-        w = weights_of(order)[("group", 1)]
-        return (fb // w) * 2 * w + g * w + fb % w
+    def place(fb, g, order, spread):
+        w = weights_of(order)
+        return g * w[("group", 1)] + sum(
+            (fb >> k) % 2 * w[("dp", s)] for k, s in enumerate(spread[:-1]))
 
     def group_of(c):
         return m if c == 0 else other
+
+    starts = [sum(p[0] for p in pn.parts[:k]) for k in range(len(pn.parts))]
 
     def w1_half(cbit, sink):
         for c in range(2):
             for t in range(nj):
                 r = mm(featt[pl.ds(pl.multiple_of(cbit * half_f, half_f), half_f), :], gp[c * nj + t])
                 for fb in range(per_core):
-                    for p, order in enumerate(pn.w_orders):
-                        p0, p1 = PART_ROWS[p], PART_ROWS[p + 1]
-                        sink(p, place(fb, group_of(c), order), t,
-                             r[fb * CH + p0 : fb * CH + p1, :])
-
-    def slot_at(p, slot, n):
-        p0, p1 = PART_ROWS[p], PART_ROWS[p + 1]
-        pr = (p1 - p0) * nj
-        return pl.ds(pl.multiple_of((n_all - 1) * nj * p0 + slot * pr, 16), n * pr)
+                    for p, (pr, order, spread) in enumerate(pn.parts):
+                        at = fb * CH + starts[p]
+                        sink(p, place(fb, group_of(c), order, spread), t, r[at : at + pr, :])
+
+    def piece_at(p, n, slot, t, size):
+        pr = pn.parts[p][0]
+        return pl.ds(pl.multiple_of(n * nj * starts[p] + slot * (nj * pr) + t * pr, 16), size * pr)
 
     def sink_send(p, j, t, v):
-        pr = PART_ROWS[p + 1] - PART_ROWS[p]
-        at = (n_all - 1) * nj * PART_ROWS[p] + j * (nj * pr) + t * pr
-        big[pl.ds(pl.multiple_of(at, 16), pr), :] = v.astype(BF16)
+        big[piece_at(p, n_all - 1, j, t, 1), :] = v.astype(BF16)
+
+    def cut_of(p, t):
+        return slice(t * CH + starts[p], t * CH + starts[p] + pn.parts[p][0])
 
     def sink_acc(p, j, t, v):
-        p0, p1 = PART_ROWS[p], PART_ROWS[p + 1]
-        logits[j, t * CH + p0 : t * CH + p1, :] = v
+        logits[j, cut_of(p, t), :] = v
 
     def w_chain(p):
-        p0, p1 = PART_ROWS[p], PART_ROWS[p + 1]
-        pr = p1 - p0
-
-        def put(slot, a):
+        def total(a, got, t):
+            return logits[a, cut_of(p, t), :] + recv[
+                piece_at(p, n_all - 1, got, t, 1), :].astype(F32)
+
+        def put(slot, a, got):
             for t in range(nj):
-                sink_send(p, slot, t, logits[a, t * CH + p0 : t * CH + p1, :])
-
-        def add(a, slot):
-            at = (n_all - 1) * nj * p0 + slot * (nj * pr)
+                sink_send(p, slot, t, total(a, got, t))
+
+        def add(a, got):
             for t in range(nj):
-                cut = slice(t * CH + p0, t * CH + p1)
-                logits[a, cut, :] = logits[a, cut, :] + recv[
-                    pl.ds(pl.multiple_of(at + t * pr, 16), pr), :].astype(F32)
-
-        return Chain(pn.w_orders[p], put, add,
-                     lambda s, n: big.at[slot_at(p, s, n)], lambda s, n: recv.at[slot_at(p, s, n)])
+                logits[a, cut_of(p, t), :] = total(a, got, t)
+
+        return Chain(pn.parts[p][1], put, add,
+                     lambda s, n: big.at[piece_at(p, n_all - 1, s, 0, n * nj)],
+                     lambda s, n: recv.at[piece_at(p, n_all - 1, s, 0, n * nj)])
 
     h2 = 256 // per_core
 
@@ -703,7 +735,7 @@
         for c in range(2):
             r = tn(hid[c * nj + cbit], ge[...])
             for fb in range(per_core):
-                sink(place(fb, group_of(c), pn.w2_order), r[fb * h2 : (fb + 1) * h2, :])
+                sink(place(fb, group_of(c), *pn.w2_part), r[fb * h2 : (fb + 1) * h2, :])
 
     def w2_send(j, v):
         send2[j] = v.astype(BF16)
@@ -711,80 +743,67 @@
     def w2_acc(j, v):
         acc2[j] = v
 
-    def w2_put(slot, a):
-        send2[slot] = acc2[a].astype(BF16)
-
-    def w2_add(a, slot):
-        acc2[a] = acc2[a] + recv2[slot].astype(F32)
-
-    chains = [w_chain(p) for p in range(len(pn.w_orders))]
-    w2_chain = Chain(pn.w2_order, w2_put, w2_add,
+    def w2_put(slot, a, got):
+        send2[slot] = (acc2[a] + recv2[got].astype(F32)).astype(BF16)
+
+    def w2_add(a, got):
+        acc2[a] = acc2[a] + recv2[got].astype(F32)
+
+    chains = [w_chain(p) for p in range(len(pn.parts))]
+    w2_chain = Chain(pn.w2_part[0], w2_put, w2_add,
                      lambda a, n: send2.at[pl.ds(a, n)], lambda a, n: recv2.at[pl.ds(a, n)])
     w1_half(1 - cb, sink_send)
     for ch in chains:
-        ch.begin(0)
+        ch.launch(0)
     w2_half(1 - cb, w2_send)
-    w2_chain.begin(0)
+    w2_chain.launch(0)
+    advance(q_chains, 2)
     w1_half(cb, sink_acc)
     w2_half(cb, w2_acc)
-    q_chain.step(2)
     every = chains + [w2_chain]
-    steps = len(pn.w2_order)
+    steps = len(rounds)
     for r in range(1, steps + 1):
-        for ch in every:
-            ch.step(r)
+        advance(every, r)
         if r + 2 <= steps:
-            q_chain.step(r + 2)
-
-    q_sum = qpt[own16 + q_chain.base]
-    gq_ref[...] = scale * (q_sum.T - positive)
-
-    def block_of(ch):
-        w = weights_of(ch.order)[("group", 1)]
-        return cb * per_core + lax.div(ch.base, 2 * w) * w + lax.rem(ch.base, w)
-
-    def ag_at(p, fb, n):
-        p0, p1 = PART_ROWS[p], PART_ROWS[p + 1]
-        pr = (p1 - p0) * nj
-        return pl.ds(pl.multiple_of(n_dp * nj * p0 + fb * pr, 16), n * pr)
+            advance(q_chains, r + 2)
+
+    for h in range(2):
+        gq_ref[:, h * he : (h + 1) * he] = scale * (
+            qpt[h, own16 + q_chains[h].base].T - positive[:, h * he : (h + 1) * he])
+
+    def block_of(spread):
+        return sum(bit(s) << k for k, s in enumerate(spread))
 
     views = []
     for p, ch in enumerate(chains):
-        p0, p1 = PART_ROWS[p], PART_ROWS[p + 1]
-        pr = p1 - p0
-        fb = block_of(ch)
+        spread = pn.parts[p][2]
+        fb = block_of(spread)
         for t in range(nj):
-            at = n_dp * nj * p0 + fb * (nj * pr) + t * pr
-            ag[pl.ds(pl.multiple_of(at, 16), pr), :] = logits[
-                ch.base, t * CH + p0 : t * CH + p1, :].astype(BF16)
-        views.append((ch, fb, functools.partial(lambda p, b, n: ag.at[ag_at(p, b, n)], p)))
-    fb2 = block_of(w2_chain)
+            ag[piece_at(p, n_dp, fb, t, 1), :] = logits[ch.base, cut_of(p, t), :].astype(BF16)
+        views.append((spread, fb, functools.partial(
+            lambda p, b, n: ag.at[piece_at(p, n_dp, b, 0, n * nj)], p)))
+    fb2 = block_of(pn.w2_part[1])
     ag2[fb2] = acc2[w2_chain.base].astype(BF16)
-    views.append((w2_chain, fb2, lambda b, n: ag2.at[pl.ds(b, n)]))
+    views.append((pn.w2_part[1], fb2, lambda b, n: ag2.at[pl.ds(b, n)]))
     live = [None] * len(views)
     for k in range(len(pn.bits)):
-        for i, (ch, fb, view) in enumerate(views):
+        for i, (spread, fb, view) in enumerate(views):
             if live[i] is not None:
                 live[i].wait()
-            back_order = [a for a in ch.order if a[0] == "dp"][::-1]
             size = 1 << k
             v = view(lax.div(fb, size) * size, size)
-            live[i] = remote(v, v, partner(*back_order[k])[1])
+            live[i] = remote(v, v, partner("dp", spread[k])[1])
             live[i].start()
     for c in live:
         c.wait()
 
     for p in range(len(chains)):
-        p0, p1 = PART_ROWS[p], PART_ROWS[p + 1]
-        pr = p1 - p0
-
         def out_rows(fb):
             for t in range(nj):
-                at = n_dp * nj * p0 + fb * (nj * pr) + t * pr
-                gw1_ref[pl.ds(pl.multiple_of(fb * CH + p0, 16), pr), t * 256 : (t + 1) * 256] = ag[
-                    pl.ds(pl.multiple_of(at, 16), pr), :]
-
-        loop(n_dp, out_rows)
+                gw1_ref[pl.ds(pl.multiple_of(fb * CH + starts[p], 16), pn.parts[p][0]),
+                        t * 256 : (t + 1) * 256] = ag[piece_at(p, n_dp, fb, t, 1), :]
+
+        loop_by(4, n_dp, out_rows)
     gw2_ref[...] = ag2[...].reshape(gw2_ref.shape)
 
 
@@ -803,7 +822,7 @@
     sends = (n_all - 1) * nj * CH
     big = -(-max(sends, (fg // 256) * pn.slab) // 16) * 16
     hp = hg // n_dp
-    n_sem = 80
+    n_sem = 96
     S = pltpu.VMEM
     loss, gq, gw1, gw2 = pl.pallas_call(
         functools.partial(fused_kernel, pn, rows),
@@ -835,7 +854,7 @@
             S((rows, width), F32),
             S((rows, emb), F32),
             S((n_dp, rows, width), F32),
-            S((n_all, emb, width // 2), F32),
+            S((2, n_all, emb // 2, width // 2), F32),
             S((rounds + 1, 2, n_dp, width), F32),
             S((rounds, 2, n_dp, width), F32),
             S((n_dp, width), F32),
@@ -845,8 +864,8 @@
             S((rows, emb), BF16),
             S((sends, 256), BF16),
             S((n_dp * nj * CH, 256), BF16),
-            S((n_all - 1, emb, width // 2), BF16),
-            S((n_all - 1, emb, width // 2), BF16),
+            S((2, n_all - 1, emb // 2, width // 2), BF16),
+            S((2, n_all - 1, emb // 2, width // 2), BF16),
             S((n_dp, hp, emb), F32),
             S((n_all - 1, hp, emb), BF16),
             S((n_all - 1, hp, emb), BF16),

time: 151 us -> 131 us (0.87)
  Pallas kernels: 149 us -> 128 us
    pallas_call x1, Pallas kernels: 145 us -> 124 us  [fused(): pl.pallas_call(functools.partial(fused_kernel, pn, rows), out_shape=(jax....]
where the time goes in v3:
time: 131 us; the launch traced here: 130 us
  Pallas kernels  128 us (98%)
    pallas_call x1, Pallas kernels, fused(): pl.pallas_call(functools.partial(fused_kernel, pn, rows), out_shape=(jax....  124 us
    pallas_call x1, Pallas kernels, widen(): pl.pallas_call(widen_kernel, grid=(parts,), out_shape=tuple((jax.ShapeDty...  4.34 us

profile of v3, /device:TPU:0, one launch (start us, length us, event | category | flops | bytes accessed | tf_op | source)
XLA Modules:
  0.0 130.4 jit_solution(11179046582468171924)
XLA Ops:
  0.6 1.3 bitcast_convert_fusion.shift_in
  1.9 124.1 %fused.1 = (f32[1,128]{1,0:T(1,128)}, f32[128,256]{1,0:T(8,128)}, bf16[2048,512]{1,0:T(8,128)(2,1)}, bf16[512,256]{1,0:T(8,128)(2,1)}) custom-call(bf16[256,256]{1,0:T(8,128)(2,1)} %queries.1, bf16[256,1024]{1,0:T(8,128)(2,1)} %items.1, bf16[2048,1024]{1,0:T(8,128)(2,1)} %corpus.1, s32[8,128]{1,0:T(8,128)} %bitcast.5, ...), custom_call_target="tpu_custom_call" | custom-call | tf_op jit(solution)/shard_map/fused/pallas_call | solution.py:827
  126.0 4.3 %widen.1 = (f32[1,128]{1,0:T(1,128)}, f32[128,256]{1,0:T(8,128)}, f32[2048,512]{1,0:T(8,128)}, f32[512,256]{1,0:T(8,128)}) custom-call(f32[1,128]{1,0:T(1,128)} %get-tuple-element.12.refs_0_, f32[128,256]{1,0:T(8,128)} %get-tuple-element.13.refs_1_, bf16[2048,512]{1,0:T(8,128)(2,1)} %get-tuple-element.14.refs_2_, bf16[512,256]{1,0:T(8,128)(2,1)} %get-tuple-element.15.refs_3_), custom_call_target="tpu_custom_call" | custom-call | tf_op jit(solution)/shard_map/widen/pallas_call | solution.py:894

commit v4 on v3

--- a/solution.py
+++ b/solution.py
@@ -301,15 +301,20 @@
         dp = lambda steps: [("dp", s) for s in steps]
         y = [("group", 1)]
         self.gather_orders = [[x] + z[::-1] + [core], z[::-1] + [x, core]]
-        self.w_gather = [z[0], x, core]
+        self.w_gathers = [[x, z[0], core], [z[0], x, core]]
+        self.phases = [dp([core, x]), dp(z[:1]) + y, dp(z[1:])]
         self.q_orders = [dp([core, x]) + y + dp(z), dp([core]) + y + dp([x]) + dp(z)]
         zn, zf = z[:1], z[1:]
-        self.parts = [
-            (48, dp([core]) + y + dp(zn + [x] + zf), z[::-1] + [x, core]),
-            (16, dp([core, x]) + y + dp(z), z[::-1] + [x, core]),
-            (32, dp([core, x]) + y + dp(z), [x] + z[::-1] + [core]),
-            (32, dp([core] + zn + [x] + zf) + y, zf[::-1] + [x] + zn + [core]),
+        far_first, x_first = z[::-1] + [x, core], [x] + z[::-1] + [core]
+        y_red = dp([core]) + y + dp(zn + [x] + zf)
+        x_red = dp([core, x]) + y + dp(z)
+        z_red = dp([core] + zn + [x] + zf) + y
+        z_gat = zf[::-1] + [x] + zn + [core]
+        self.groups = [
+            [(32, y_red, far_first), (16, x_red, far_first), (16, z_red, z_gat)],
+            [(16, y_red, far_first), (32, x_red, x_first), (16, z_red, z_gat)],
         ]
+        self.parts = self.groups[0] + self.groups[1]
         self.w2_part = (dp([core] + zn + [x]) + y + dp(zf), z[::-1] + [x, core])
         self.bits = bits
 
@@ -335,6 +340,18 @@
     core, xbit = pn.bits[0], pn.bits[1]
     rounds = [("dp", s) for s in pn.bits] + [("group", 1)]
     count = iter(range(1000))
+
+    def across(subset):
+        to = {}
+        for axis, step in subset:
+            at = to.get(axis, lax.axis_index(axis))
+            to[axis] = at + step - 2 * step * lax.rem(lax.div(lax.axis_index(axis), step), 2)
+        return to
+
+    def subsets(phase):
+        return [[r for k, r in enumerate(phase) if mask >> k & 1] for mask in range(1, 1 << len(phase))]
+
+    met = [across(sub) for phase in pn.phases for sub in subsets(phase)]
     lcount = iter(range(100))
 
     def bit(step):
@@ -362,7 +379,7 @@
     c_mine = local(items.at[pl.ds(pl.multiple_of(m * quota, quota), quota)], mine.at[0:quota])
     c_w1 = local(w1, w1v.at[0])
     c_w2 = local(w2, w2v.at[0])
-    greet([partner(a, b)[1] for a, b in rounds])
+    greet(met)
 
     class Spread:
         def __init__(self, first, follow, n):
@@ -381,26 +398,26 @@
                     c.start()
                 self.k += 1
 
-    n_piece = 1 << len(pn.w_gather)
-    e = sum(bit(s) << k for k, s in enumerate(pn.w_gather))
+    n_piece = 1 << len(pn.w_gathers[0])
+    es = [sum(bit(s) << k for k, s in enumerate(gather)) for gather in pn.w_gathers]
     q1, q2 = fg // n_piece, hg // 2 // n_piece
 
-    def w_rows(half, size):
-        base = lax.div(e, size) * size
+    def w_rows(u, half, size):
+        base = lax.div(es[u], size) * size
         return (pl.ds(pl.multiple_of(half * fg + base * q1, q1), size * q1),
                 pl.ds(pl.multiple_of(half * (hg // 2) + base * q2, q2), size * q2))
 
-    def w_spread(half, far_half):
-        a, b = w_rows(far_half, 1)
+    def w_spread(u, half, far_half):
+        a, b = w_rows(u, far_half, 1)
 
         def follow(k):
-            at1, at2 = w_rows(half, 1 << k)
-            to = partner("dp", pn.w_gather[k])[1]
+            at1, at2 = w_rows(u, half, 1 << k)
+            to = partner("dp", pn.w_gathers[u][k])[1]
             return [remote(w1v.at[1, at1], w1v.at[1, at1], to),
                     remote(w2v.at[1, at2], w2v.at[1, at2], to)]
 
         return Spread([remote(w1.at[a], w1v.at[1, a], ypeer), remote(w2.at[b], w2v.at[1, b], ypeer)],
-                      follow, len(pn.w_gather))
+                      follow, len(pn.w_gathers[u]))
 
     def q_spread(g):
         def follow(k):
@@ -409,7 +426,7 @@
 
         return Spread(follow(0), lambda k: follow(k + 1), len(pn.bits) - 1)
 
-    ws = [w_spread(m, other), w_spread(other, m)]
+    ws = [w_spread(0, m, other), w_spread(1, other, m)]
     for c in c_q:
         c.wait()
     qs = [q_spread(0), q_spread(1)]
@@ -445,9 +462,9 @@
     ws[1].go()
     loop(chunks, lambda k: far_copy(k).start())
     loop(chunks, lambda k: pick(m, k, mine, rows_at(k)))
-    qs[1].go()
     ws[0].go()
     qs[0].go()
+    ws[1].go()
     bias[0:quota, :] = jnp.zeros((quota, width), F32)
 
     def put_bias(k):
@@ -458,7 +475,6 @@
     c_mine.wait()
     c_w1.wait()
     c_w2.wait()
-    ws[1].go()
 
     nj = hg // 256
 
@@ -473,15 +489,23 @@
 
     tower_add(0, rows, mine, m, 0, True)
     qs[1].go()
-    qs[0].go()
+
+    hb = CH // 2
 
     def turn(src, half, n):
         at = pl.multiple_of(n * 256, 256)
-        featt[pl.ds(pl.multiple_of(half * fg + at, 256), 256), :] = src[:, pl.ds(at, 256)].T
-
+        block = src[:, pl.ds(at, 256)].T
+        for b in range(256 // CH):
+            for k in range(2):
+                row = half * fg + k * (fg // 2) + (n * (256 // CH) + b) * hb
+                featt[pl.ds(pl.multiple_of(row, hb), hb), :] = block[
+                    b * CH + k * hb : b * CH + (k + 1) * hb, :]
+
+    loop(fg // 256, lambda n: turn(mine, m, n))
     ws[0].go()
-    loop(fg // 256, lambda n: turn(mine, m, n))
     ws[1].go()
+    qs[0].go()
+    qs[1].go()
     ws[0].go()
     tower_add(0, rows, mine, m, 1, True)
     ws[1].go()
@@ -554,19 +578,25 @@
                 qpt[h, shard_of(i, g, h)] = part[
                     h * he : (h + 1) * he, g * half_q : (g + 1) * half_q]
 
-    for r, (axis, step) in enumerate(rounds):
-        copy = remote(stats.at[r], arrived.at[r], partner(axis, step)[1])
-        copy.start()
-        if r < 4:
-            loop_by(2, tiles // 4, lambda i: query_part(r * (tiles // 4) + i))
+    slot = 0
+    for ph, phase in enumerate(pn.phases):
+        copies = []
+        for sub in subsets(phase):
+            copies.append(remote(stats.at[ph], arrived.at[slot + len(copies)], across(sub)))
+            copies[-1].start()
+        if ph < 2:
+            loop_by(4, tiles // 2, lambda i: query_part(ph * (tiles // 2) + i))
         else:
             loop(fg // 256, lambda n: turn(peer, other, n))
-        copy.wait()
-        m0, s0, m1, s1 = stats[r, 0], stats[r, 1], arrived[r, 0], arrived[r, 1]
-        top = jnp.maximum(m0, m1)
-        stats[r + 1, 0] = top
-        stats[r + 1, 1] = s0 * jnp.exp(m0 - top) + s1 * jnp.exp(m1 - top)
-    last = len(rounds)
+        for c in copies:
+            c.wait()
+        held = [(stats[ph, 0], stats[ph, 1])] + [
+            (arrived[slot + k, 0], arrived[slot + k, 1]) for k in range(len(copies))]
+        slot += len(copies)
+        top = functools.reduce(jnp.maximum, [a for a, _ in held])
+        stats[ph + 1, 0] = top
+        stats[ph + 1, 1] = sum(b * jnp.exp(a - top) for a, b in held)
+    last = len(pn.phases)
     total_ref[...] = stats[last, 0] + jnp.log(stats[last, 1])
     fac[...] = jnp.exp(stats[0, 0] - total_ref[...])
 
@@ -690,13 +720,16 @@
 
     starts = [sum(p[0] for p in pn.parts[:k]) for k in range(len(pn.parts))]
 
-    def w1_half(cbit, sink):
+    def w1_half(cbit, k, sink):
+        own = range(k * len(pn.groups[0]), (k + 1) * len(pn.groups[0]))
+        span = pl.ds(pl.multiple_of(cbit * half_f + k * (half_f // 2), half_f // 2), half_f // 2)
         for c in range(2):
             for t in range(nj):
-                r = mm(featt[pl.ds(pl.multiple_of(cbit * half_f, half_f), half_f), :], gp[c * nj + t])
+                r = mm(featt[span, :], gp[c * nj + t])
                 for fb in range(per_core):
-                    for p, (pr, order, spread) in enumerate(pn.parts):
-                        at = fb * CH + starts[p]
+                    for p in own:
+                        pr, order, spread = pn.parts[p]
+                        at = fb * hb + starts[p] - k * hb
                         sink(p, place(fb, group_of(c), order, spread), t, r[at : at + pr, :])
 
     def piece_at(p, n, slot, t, size):
@@ -752,50 +785,73 @@
     chains = [w_chain(p) for p in range(len(pn.parts))]
     w2_chain = Chain(pn.w2_part[0], w2_put, w2_add,
                      lambda a, n: send2.at[pl.ds(a, n)], lambda a, n: recv2.at[pl.ds(a, n)])
-    w1_half(1 - cb, sink_send)
-    for ch in chains:
-        ch.launch(0)
+    teams = [chains[:3], chains[3:] + [w2_chain]]
+    for k in range(2):
+        w1_half(1 - cb, k, sink_send)
+        for ch in chains[3 * k : 3 * k + 3]:
+            ch.launch(0)
     w2_half(1 - cb, w2_send)
     w2_chain.launch(0)
     advance(q_chains, 2)
-    w1_half(cb, sink_acc)
+    w1_half(cb, 0, sink_acc)
+    advance(teams[0], 1)
+    w1_half(cb, 1, sink_acc)
     w2_half(cb, w2_acc)
+    advance(teams[1], 1)
+    advance(q_chains, 3)
     every = chains + [w2_chain]
     steps = len(rounds)
-    for r in range(1, steps + 1):
-        advance(every, r)
+    for r in range(2, steps):
+        for team in teams:
+            advance(team, r)
         if r + 2 <= steps:
             advance(q_chains, r + 2)
+
+    def block_of(spread):
+        return sum(bit(s) << k for k, s in enumerate(spread))
+
+    def w1_view(p, b, n):
+        return ag.at[piece_at(p, n_dp, b, 0, n * nj)]
+
+    def start_gather(i):
+        p = every.index(i)
+        if i is w2_chain:
+            spread = pn.w2_part[1]
+            fb = block_of(spread)
+            ag2[fb] = acc2[i.base].astype(BF16)
+            return spread, fb, lambda b, n: ag2.at[pl.ds(b, n)]
+        spread = pn.parts[p][2]
+        fb = block_of(spread)
+        for t in range(nj):
+            ag[piece_at(p, n_dp, fb, t, 1), :] = logits[i.base, cut_of(p, t), :].astype(BF16)
+        return spread, fb, functools.partial(w1_view, p)
+
+    def share(one, k):
+        spread, fb, view = one
+        size = 1 << k
+        v = view(lax.div(fb, size) * size, size)
+        c = remote(v, v, partner("dp", spread[k])[1])
+        c.start()
+        return c
+
+    live, views = [], []
+    for team in teams:
+        group = []
+        for ch in team:
+            ch.finish()
+            group.append(start_gather(ch))
+        views.append(group)
+        live.append([share(one, 0) for one in group])
+    for k in range(1, len(pn.bits) + 1):
+        for i, group in enumerate(views):
+            for j, one in enumerate(group):
+                live[i][j].wait()
+                if k < len(pn.bits):
+                    live[i][j] = share(one, k)
 
     for h in range(2):
         gq_ref[:, h * he : (h + 1) * he] = scale * (
             qpt[h, own16 + q_chains[h].base].T - positive[:, h * he : (h + 1) * he])
-
-    def block_of(spread):
-        return sum(bit(s) << k for k, s in enumerate(spread))
-
-    views = []
-    for p, ch in enumerate(chains):
-        spread = pn.parts[p][2]
-        fb = block_of(spread)
-        for t in range(nj):
-            ag[piece_at(p, n_dp, fb, t, 1), :] = logits[ch.base, cut_of(p, t), :].astype(BF16)
-        views.append((spread, fb, functools.partial(
-            lambda p, b, n: ag.at[piece_at(p, n_dp, b, 0, n * nj)], p)))
-    fb2 = block_of(pn.w2_part[1])
-    ag2[fb2] = acc2[w2_chain.base].astype(BF16)
-    views.append((pn.w2_part[1], fb2, lambda b, n: ag2.at[pl.ds(b, n)]))
-    live = [None] * len(views)
-    for k in range(len(pn.bits)):
-        for i, (spread, fb, view) in enumerate(views):
-            if live[i] is not None:
-                live[i].wait()
-            size = 1 << k
-            v = view(lax.div(fb, size) * size, size)
-            live[i] = remote(v, v, partner("dp", spread[k])[1])
-            live[i].start()
-    for c in live:
-        c.wait()
 
     for p in range(len(chains)):
         def out_rows(fb):
@@ -822,7 +878,7 @@
     sends = (n_all - 1) * nj * CH
     big = -(-max(sends, (fg // 256) * pn.slab) // 16) * 16
     hp = hg // n_dp
-    n_sem = 96
+    n_sem = 128
     S = pltpu.VMEM
     loss, gq, gw1, gw2 = pl.pallas_call(
         functools.partial(fused_kernel, pn, rows),
@@ -856,7 +912,7 @@
             S((n_dp, rows, width), F32),
             S((2, n_all, emb // 2, width // 2), F32),
             S((rounds + 1, 2, n_dp, width), F32),
-            S((rounds, 2, n_dp, width), F32),
+            S((sum((1 << len(p)) - 1 for p in pn.phases), 2, n_dp, width), F32),
             S((n_dp, width), F32),
             S((n_dp, width), F32),
             S((feats, rows), BF16),
@@ -888,7 +944,7 @@
 
 
 def widen(loss, *grads):
-    parts = 4
+    parts = 2
     specs = [pl.BlockSpec(loss.shape, lambda i: (0, 0))] + [
         pl.BlockSpec((x.shape[0] // parts, x.shape[1]), lambda i: (i, 0)) for x in grads]
     loss, *grads = pl.pallas_call(

time: 131 us -> 120 us (0.916)
  Pallas kernels: 128 us -> 118 us
    pallas_call x1, Pallas kernels: 124 us -> 115 us  [fused(): pl.pallas_call(functools.partial(fused_kernel, pn, rows), out_shape=(jax....]
where the time goes in v4:
time: 120 us
  Pallas kernels  118 us (98%)
  other arithmetic  1.28 us (1%)
    pallas_call x1, Pallas kernels, fused(): pl.pallas_call(functools.partial(fused_kernel, pn, rows), out_shape=(jax....  115 us
    pallas_call x1, Pallas kernels, widen(): pl.pallas_call(widen_kernel, grid=(parts,), out_shape=tuple((jax.ShapeDty...  3.67 us

profile of v4, /device:TPU:0, one launch (start us, length us, event | category | flops | bytes accessed | tf_op | source)
XLA Modules:
  0.0 120.3 jit_solution(17032142163690812175)
XLA Ops:
  0.6 1.3 %bitcast_convert_fusion.shift_in = f32[8,128]{1,0:T(8,128)} fusion(bf16[1024]{0:T(1024)(128)(2,1)} %param.11), kind=kLoop, calls=%fused_computation | loop fusion | flops 1024 | bytes 6144 | tf_op jit(solution)/shard_map/reshape | solution.py:876
  1.9 114.7 %fused.1 = (f32[1,128]{1,0:T(1,128)}, f32[128,256]{1,0:T(8,128)}, bf16[2048,512]{1,0:T(8,128)(2,1)}, bf16[512,256]{1,0:T(8,128)(2,1)}) custom-call(bf16[256,256]{1,0:T(8,128)(2,1)} %queries.1, bf16[256,1024]{1,0:T(8,128)(2,1)} %items.1, bf16[2048,1024]{1,0:T(8,128)(2,1)} %corpus.1, s32[8,128]{1,0:T(8,128)} %bitcast.5, ...), custom_call_target="tpu_custom_call" | custom-call | tf_op jit(solution)/shard_map/fused/pallas_call | solution.py:883
  116.6 3.7 %widen.1 = (f32[1,128]{1,0:T(1,128)}, f32[128,256]{1,0:T(8,128)}, f32[2048,512]{1,0:T(8,128)}, f32[512,256]{1,0:T(8,128)}) custom-call(f32[1,128]{1,0:T(1,128)} %get-tuple-element.12.refs_0_, f32[128,256]{1,0:T(8,128)} %get-tuple-element.13.refs_1_, bf16[2048,512]{1,0:T(8,128)(2,1)} %get-tuple-element.14.refs_2_, bf16[512,256]{1,0:T(8,128)(2,1)} %get-tuple-element.15.refs_3_), custom_call_target="tpu_custom_call" | custom-call | tf_op jit(solution)/shard_map/widen/pallas_call | solution.py:950

commit v5 on v4

--- a/solution.py
+++ b/solution.py
@@ -315,7 +315,7 @@
             [(16, y_red, far_first), (32, x_red, x_first), (16, z_red, z_gat)],
         ]
         self.parts = self.groups[0] + self.groups[1]
-        self.w2_part = (dp([core] + zn + [x]) + y + dp(zf), z[::-1] + [x, core])
+        self.w2_part = (y_red, far_first)
         self.bits = bits
 
 
@@ -326,7 +326,7 @@
 def fused_kernel(pn, rows, queries, items, corpus, ids_in, shift_in, w1, w2,
                  loss_ref, gq_ref, gw1_ref, gw2_ref,
                  big, q_all, w1v, w2v, mine, peer, far, hot, ids_v, shift_v, pre, hid, emb, nrm, nrms, nrm_t,
-                 bias, hat, logits, qpt, stats, arrived, total_ref, fac, featt, gp, ge,
+                 bias, hat, logits, qpt, stats, lse, arrived, total_ref, fac, featt, gp, ge,
                  recv, ag, qsend, qrecv, acc2, send2, recv2, ag2, lsem, ssem, rsem):
     n_dp, width, fg, hg, slab = pn.n_dp, pn.query_rows, pn.fg, pn.hg, pn.slab
     quota, e_dim = pn.quota, pn.emb
@@ -373,7 +373,7 @@
     tiles = n_dp
 
     c_q = [local(queries.at[g * quota : (g + 1) * quota], q_all.at[g, poss[g]]) for g in range(2)]
-    c_meta = [local(ids_in, ids_v), local(shift_in, shift_v)]
+    c_meta = [local(ids_in, ids_v)]
     c_slab = [local(corpus.at[:, n * 256 : (n + 1) * 256], big.at[n * slab : (n + 1) * slab])
               for n in range(fg // 256)]
     c_mine = local(items.at[pl.ds(pl.multiple_of(m * quota, quota), quota)], mine.at[0:quota])
@@ -465,6 +465,7 @@
     ws[0].go()
     qs[0].go()
     ws[1].go()
+    shift_v[...] = shift_in[...].astype(F32)
     bias[0:quota, :] = jnp.zeros((quota, width), F32)
 
     def put_bias(k):
@@ -578,11 +579,12 @@
                 qpt[h, shard_of(i, g, h)] = part[
                     h * he : (h + 1) * he, g * half_q : (g + 1) * half_q]
 
+    lse[0] = stats[0, 0] + jnp.log(stats[0, 1])
     slot = 0
     for ph, phase in enumerate(pn.phases):
         copies = []
         for sub in subsets(phase):
-            copies.append(remote(stats.at[ph], arrived.at[slot + len(copies)], across(sub)))
+            copies.append(remote(lse.at[ph], arrived.at[slot + len(copies)], across(sub)))
             copies[-1].start()
         if ph < 2:
             loop_by(4, tiles // 2, lambda i: query_part(ph * (tiles // 2) + i))
@@ -590,14 +592,11 @@
             loop(fg // 256, lambda n: turn(peer, other, n))
         for c in copies:
             c.wait()
-        held = [(stats[ph, 0], stats[ph, 1])] + [
-            (arrived[slot + k, 0], arrived[slot + k, 1]) for k in range(len(copies))]
+        held = [lse[ph]] + [arrived[slot + k] for k in range(len(copies))]
         slot += len(copies)
-        top = functools.reduce(jnp.maximum, [a for a, _ in held])
-        stats[ph + 1, 0] = top
-        stats[ph + 1, 1] = sum(b * jnp.exp(a - top) for a, b in held)
-    last = len(pn.phases)
-    total_ref[...] = stats[last, 0] + jnp.log(stats[last, 1])
+        top = functools.reduce(jnp.maximum, held)
+        lse[ph + 1] = top + jnp.log(sum(jnp.exp(a - top) for a in held))
+    total_ref[...] = lse[len(pn.phases)]
     fac[...] = jnp.exp(stats[0, 0] - total_ref[...])
 
     class Chain:
@@ -873,7 +872,7 @@
     n_all = 2 * n_dp
     rounds = n_all.bit_length() - 1
     ids = sample_ids.reshape(-1, CH)
-    shifts = sample_shift.astype(F32).reshape(-1, CH)
+    shifts = sample_shift.reshape(-1, CH)
     half = feats // 2
     sends = (n_all - 1) * nj * CH
     big = -(-max(sends, (fg // 256) * pn.slab) // 16) * 16
@@ -888,7 +887,7 @@
             jax.ShapeDtypeStruct((feats, hg), BF16),
             jax.ShapeDtypeStruct((hg, emb), BF16),
         ),
-        in_specs=[ANY] * 7,
+        in_specs=[ANY] * 4 + [VMEM] + [ANY] * 2,
         out_specs=(VMEM,) * 4,
         scratch_shapes=[
             S((big, 256), BF16),
@@ -911,8 +910,9 @@
             S((rows, emb), F32),
             S((n_dp, rows, width), F32),
             S((2, n_all, emb // 2, width // 2), F32),
-            S((rounds + 1, 2, n_dp, width), F32),
-            S((sum((1 << len(p)) - 1 for p in pn.phases), 2, n_dp, width), F32),
+            S((1, 2, n_dp, width), F32),
+            S((len(pn.phases) + 1, n_dp, width), F32),
+            S((sum((1 << len(p)) - 1 for p in pn.phases), n_dp, width), F32),
             S((n_dp, width), F32),
             S((n_dp, width), F32),
             S((feats, rows), BF16),

time: 120 us -> 118 us (0.983)
  other arithmetic: 1.28 us -> 0 us
    pallas_call x1, Pallas kernels: 115 us -> 113 us  [fused(): pl.pallas_call(functools.partial(fused_kernel, pn, rows), out_shape=(jax....]
    reshape x1 -> x0, other arithmetic: 1.28 us -> none  [fused(): shifts = sample_shift.astype(F32).reshape(-1, CH)]
where the time goes in v5:
time: 118 us
  Pallas kernels  117 us (99%)
    pallas_call x1, Pallas kernels, fused(): pl.pallas_call(functools.partial(fused_kernel, pn, rows), out_shape=(jax....  113 us
    pallas_call x1, Pallas kernels, widen(): pl.pallas_call(widen_kernel, grid=(parts,), out_shape=tuple((jax.ShapeDty...  3.67 us

profile of v5, /device:TPU:0, one launch (start us, length us, event | category | flops | bytes accessed | tf_op | source)
XLA Modules:
  0.0 117.5 jit_solution(4882513044894990006)
XLA Ops:
  0.6 113.2 %fused.1 = (f32[1,128]{1,0:T(1,128)}, f32[128,256]{1,0:T(8,128)}, bf16[2048,512]{1,0:T(8,128)(2,1)}, bf16[512,256]{1,0:T(8,128)(2,1)}) custom-call(bf16[256,256]{1,0:T(8,128)(2,1)} %queries.1, bf16[256,1024]{1,0:T(8,128)(2,1)} %items.1, bf16[2048,1024]{1,0:T(8,128)(2,1)} %corpus.1, s32[8,128]{1,0:T(8,128)} %bitcast.3, bf16[8,128]{1,0:T(8,128)(2,1)} %bitcast.4, ...), custom_call_target="tpu_custom_call" | custom-call | tf_op jit(solution)/shard_map/fused/pallas_call | solution.py:882
  113.9 3.7 %widen.1 = (f32[1,128]{1,0:T(1,128)}, f32[128,256]{1,0:T(8,128)}, f32[2048,512]{1,0:T(8,128)}, f32[512,256]{1,0:T(8,128)}) custom-call(f32[1,128]{1,0:T(1,128)} %get-tuple-element.12.refs_0_, f32[128,256]{1,0:T(8,128)} %get-tuple-element.13.refs_1_, bf16[2048,512]{1,0:T(8,128)(2,1)} %get-tuple-element.14.refs_2_, bf16[512,256]{1,0:T(8,128)(2,1)} %get-tuple-element.15.refs_3_), custom_call_target="tpu_custom_call" | custom-call | tf_op jit(solution)/shard_map/widen/pallas_call | solution.py:950

commit v6 on v5

--- a/solution.py
+++ b/solution.py
@@ -659,20 +659,25 @@
 
     q_chains = [q_chain(0), q_chain(1)]
 
-    def scale_q(i):
-        f = fac[pl.ds(i, 1), :]
+    def scaled(i, g, h):
+        f = fac[pl.ds(i, 1), :][:, g * half_q : (g + 1) * half_q]
+        return qpt[h, shard_of(i, g, h)] * f
+
+    def q_first(h, k):
+        i = (1 - cb) * (tiles // 2) + k
+        for g in range(2):
+            qsend[h, shard_of(i, g, h) - (1 - cb) * n_dp] = scaled(i, g, h).astype(BF16)
+
+    def q_keep(k):
+        i = cb * (tiles // 2) + k
         for g in range(2):
             for h in range(2):
-                j = shard_of(i, g, h)
-                qpt[h, j] = qpt[h, j] * f[:, g * half_q : (g + 1) * half_q]
-
-    def q_first(h, j):
-        qsend[h, j] = qpt[h, (1 - cb) * n_dp + j].astype(BF16)
-
-    loop_by(4, tiles, scale_q)
+                qpt[h, shard_of(i, g, h)] = scaled(i, g, h)
+
     for h in range(2):
-        loop_by(4, n_dp, functools.partial(q_first, h))
+        loop_by(4, tiles // 2, functools.partial(q_first, h))
         q_chains[h].launch(0)
+    loop_by(4, tiles // 2, q_keep)
 
     hat[...] = jnp.zeros_like(hat)
 

time: 118 us -> 118 us (level)
  no operation moved by 1% of the time
where the time goes in v6:
time: 118 us; the launch traced here: 117 us
  Pallas kernels  117 us (99%)
    pallas_call x1, Pallas kernels, fused(): pl.pallas_call(functools.partial(fused_kernel, pn, rows), out_shape=(jax....  113 us
    pallas_call x1, Pallas kernels, widen(): pl.pallas_call(widen_kernel, grid=(parts,), out_shape=tuple((jax.ShapeDty...  3.67 us

profile of v6, /device:TPU:0, one launch (start us, length us, event | category | flops | bytes accessed | tf_op | source)
XLA Modules:
  0.0 117.4 jit_solution(16828038962736811085)
XLA Ops:
  0.6 113.0 %fused.1 = (f32[1,128]{1,0:T(1,128)}, f32[128,256]{1,0:T(8,128)}, bf16[2048,512]{1,0:T(8,128)(2,1)}, bf16[512,256]{1,0:T(8,128)(2,1)}) custom-call(bf16[256,256]{1,0:T(8,128)(2,1)} %queries.1, bf16[256,1024]{1,0:T(8,128)(2,1)} %items.1, bf16[2048,1024]{1,0:T(8,128)(2,1)} %corpus.1, s32[8,128]{1,0:T(8,128)} %bitcast.3, bf16[8,128]{1,0:T(8,128)(2,1)} %bitcast.4, ...), custom_call_target="tpu_custom_call" | custom-call | tf_op jit(solution)/shard_map/fused/pallas_call | solution.py:887
  113.7 3.7 %widen.1 = (f32[1,128]{1,0:T(1,128)}, f32[128,256]{1,0:T(8,128)}, f32[2048,512]{1,0:T(8,128)}, f32[512,256]{1,0:T(8,128)}) custom-call(f32[1,128]{1,0:T(1,128)} %get-tuple-element.12.refs_0_, f32[128,256]{1,0:T(8,128)} %get-tuple-element.13.refs_1_, bf16[2048,512]{1,0:T(8,128)(2,1)} %get-tuple-element.14.refs_2_, bf16[512,256]{1,0:T(8,128)(2,1)} %get-tuple-element.15.refs_3_), custom_call_target="tpu_custom_call" | custom-call | tf_op jit(solution)/shard_map/widen/pallas_call | solution.py:955
